TPU v7x, 32 devices: a whole 2x2x4 slice. The times are simulated.
32 devices in a mesh: row: 2 (over x), col: 4 (over z), gz: 4 (over y, core).
Axes of the slice: x: 2, y: 2, z: 4, core: 2. Of those that a mesh axis runs over, the one named last changes fastest.
Arguments:
- density_matrix: bfloat16 [8192, 8192], P('row', 'col'), may hold values from -24 to 24
- block_pattern: int32 [128, 128], P('row', 'col'), may hold values from 0 to 1, as said below
- tile_lists: int32 [32, 16], replicated, may hold values from 0 to 127, as said below
- basis_values: bfloat16 [2, 4, 4, 1024, 384], P('row', 'col', 'gz'), may hold values from -0.09375 to 0.09375
- core_density: float32 [4, 32, 96], P('row', 'col', 'gz'), may hold values from 0.5 to 4
- orbitals: float32 [8192, 128], P(('col', 'gz')), may hold values from -6 to 6
Outputs:
- hamiltonian: float32 [8192, 8192], P('row', ('col', 'gz'))
- applied: float32 [8192, 128], P(('row', 'col', 'gz'))
Inputs may be any that keep to these rules, and one draw needn't show every extreme that they name: `block_pattern`: Symmetric, with ones on the diagonal. `tile_lists`: each row is increasing and holds exactly 4 block ids from every run of 32 ids that starts at a multiple of 32.
All inputs are finite; a program needn't handle non-finite values.
Results may differ from a plain program's by a relative error of at most 0.00048.
Values may be sent and summed in bfloat16 or wider, within the bound.
A program may use at most 256 MiB of HBM per device.

v0:
```python
import jax
import jax.numpy as jnp
from jax import lax
from jax.sharding import PartitionSpec as P

pbe_kappa = 0.804
pbe_mu = 0.2195149727645171
exch_const = 0.75 * (3.0 / 3.141592653589793) ** (1.0 / 3.0)
grad_scale = 4.0 * (3.0 * 3.141592653589793**2) ** (2.0 / 3.0)
density_floor = 0.2
spacing = 0.125


def with_halo(cells, sides, width):
    for axis, dim in sides:
        count = lax.axis_size(axis)
        head = lax.slice_in_dim(cells, 0, width, axis=dim)
        tail = lax.slice_in_dim(cells, cells.shape[dim] - width, cells.shape[dim], axis=dim)
        cells = jnp.concatenate(
            [
                lax.ppermute(tail, axis, [(i, (i + 1) % count) for i in range(count)]),
                cells,
                lax.ppermute(head, axis, [((i + 1) % count, i) for i in range(count)]),
            ],
            axis=dim,
        )
    return cells


def energy(density, grad_square):
    scaled = grad_square / (grad_scale * density ** (8.0 / 3.0))
    enhance = 1.0 + pbe_kappa - pbe_kappa / (1.0 + pbe_mu * scaled / pbe_kappa)
    return -exch_const * density ** (4.0 / 3.0) * enhance


def total_energy(density, grad_square):
    return jnp.sum(energy(density, grad_square))


def centered(grid_values, direction):
    higher = [slice(1, -1), slice(1, -1), slice(1, -1)]
    lesser = [slice(1, -1), slice(1, -1), slice(1, -1)]
    higher[direction] = slice(2, None)
    lesser[direction] = slice(None, -2)
    return (grid_values[tuple(higher)] - grid_values[tuple(lesser)]) / (2.0 * spacing)


def potential_twice(density):
    padded = with_halo(density, (("row", 0), ("col", 1), ("gz", 2)), 1)
    gradients = [centered(padded, direction) for direction in range(3)]
    grad_square = (
        gradients[0] * gradients[0] + gradients[1] * gradients[1] + gradients[2] * gradients[2]
    )
    first, second = jax.grad(total_energy, argnums=(0, 1))(density, grad_square)
    fluxes = jnp.stack([2.0 * second * gradients[direction] for direction in range(3)])
    flux_ext = with_halo(fluxes, (("row", 1), ("col", 2), ("gz", 3)), 1)
    divergence = centered(flux_ext[0], 0) + centered(flux_ext[1], 1) + centered(flux_ext[2], 2)
    return first - divergence


def shards(density_matrix, block_pattern, tile_lists, basis_values, core_density, orbitals):
    row_count = lax.axis_size("row")
    column_count = lax.axis_size("col")
    depth_count = lax.axis_size("gz")
    row_index = lax.axis_index("row")
    column_index = lax.axis_index("col")
    depth_index = lax.axis_index("gz")
    row_blocks, column_blocks = block_pattern.shape
    block_size = density_matrix.shape[0] // row_blocks
    listed = tile_lists.shape[1]
    per_row = listed // row_count
    per_column = listed // column_count
    width = listed * block_size
    block_area = block_size * block_size
    slab_lists = tile_lists.reshape(row_count, column_count, depth_count, listed)
    slab_lists = lax.dynamic_index_in_dim(slab_lists, depth_index, axis=2, keepdims=False)
    mine_rows = (
        lax.dynamic_slice_in_dim(slab_lists, row_index * per_row, per_row, 2)
        - row_index * row_blocks
    )
    mine_cols = (
        lax.dynamic_slice_in_dim(slab_lists, column_index * per_column, per_column, 2)
        - column_index * column_blocks
    )
    block_ids = (mine_rows[:, :, :, None] * column_blocks + mine_cols[:, :, None, :]).reshape(-1)
    pattern_flat = block_pattern.reshape(-1)
    stored = density_matrix.reshape(row_blocks, block_size, column_blocks, block_size)
    stored = stored.transpose(0, 2, 1, 3).reshape(row_blocks * column_blocks, block_area)
    stored = stored * pattern_flat.astype(jnp.bfloat16)[:, None]
    outgoing = jnp.take(stored, block_ids, axis=0).reshape(
        row_count, column_count, per_row * per_column, block_area
    )
    flat_out = outgoing.reshape(row_count * column_count, per_row * per_column, block_area)
    incoming = lax.all_to_all(flat_out, ("row", "col"), split_axis=0, concat_axis=0, tiled=True)
    tile_matrix = incoming.reshape(
        row_count, column_count, per_row, per_column, block_size, block_size
    )
    tile_matrix = tile_matrix.transpose(0, 2, 4, 1, 3, 5).reshape(width, width)
    phi_tile = basis_values.reshape(width, -1)
    product = jnp.dot(tile_matrix, phi_tile, preferred_element_type=jnp.float32)
    rho_tile = jnp.sum(phi_tile * product, axis=0).reshape(core_density.shape)
    density = jnp.maximum(rho_tile + core_density, density_floor)
    field = potential_twice(density)
    weighted = (phi_tile * field.reshape(1, -1)).astype(jnp.bfloat16)
    local_ham = lax.dot_general(
        weighted, phi_tile, (((1,), (1,)), ((), ())), preferred_element_type=jnp.float32
    )
    returning = local_ham.reshape(
        row_count, per_row, block_size, column_count, per_column, block_size
    )
    returning = returning.transpose(0, 3, 1, 4, 2, 5).reshape(
        row_count, column_count, per_row * per_column, block_area
    )
    flat_back = returning.reshape(row_count * column_count, per_row * per_column, block_area)
    arrived = lax.all_to_all(flat_back, ("row", "col"), split_axis=0, concat_axis=0, tiled=True)
    owned = jnp.zeros((row_blocks * column_blocks, block_area), jnp.float32)
    owned = owned.at[block_ids].add(arrived.reshape(-1, block_area))
    owned = owned * pattern_flat.astype(jnp.float32)[:, None]
    dense = owned.reshape(row_blocks, column_blocks, block_size, block_size)
    dense = dense.transpose(0, 2, 1, 3).reshape(row_blocks * block_size, column_blocks * block_size)
    share = lax.psum_scatter(dense, "gz", scatter_dimension=1, tiled=True)
    terms = jnp.dot(
        share, orbitals, precision=lax.Precision.HIGHEST, preferred_element_type=jnp.float32
    )
    applied = lax.psum_scatter(terms, ("col", "gz"), scatter_dimension=0, tiled=True)
    return (share, applied)


def solution(mesh):
    placed = (
        P("row", "col"),
        P("row", "col"),
        P(),
        P("row", "col", "gz", None, None),
        P("row", "col", "gz"),
        P(("col", "gz"), None),
    )
    return jax.shard_map(
        shards,
        mesh=mesh,
        in_specs=placed,
        out_specs=(P("row", ("col", "gz")), P(("row", "col", "gz"), None)),
        check_vma=False,
    )
```

profile of v0, /device:TPU:0, one launch (start us, length us, event | category | flops | bytes accessed | tf_op | source)
XLA Modules:
  0.0 892.1 jit_solution(9858242320398911972)
XLA Ops:
  7.2 0.8 copy.16
  8.5 0.8 fusion.17
  9.5 47.7 %reshape.123 = bf16[64,64,32,64]{3,2,1,0:T(8,128)(2,1)} reshape(bf16[4096,2048]{1,0:T(8,128)(2,1)} %param.6) | data formatting | bytes 33554432 | tf_op jit(solution)/shard_map/reshape | solution.py:87
  57.2 23.1 %copy.26 = bf16[64,64,32,64]{3,1,2,0:T(8,128)(2,1)} copy(bf16[64,64,32,64]{3,2,1,0:T(8,128)(2,1)} %reshape.123) | data formatting | bytes 33554432 | tf_op jit(solution)/shard_map/reshape | solution.py:87
  80.3 44.0 %reshape.124 = bf16[2048,4096]{1,0:T(8,128)(2,1)} reshape(bf16[64,32,64,64]{3,2,1,0:T(8,128)(2,1)} %bitcast.57) | data formatting | bytes 33554432 | tf_op jit(solution)/shard_map/reshape | solution.py:88
  124.3 14.0 %broadcast_multiply_fusion.1 = bf16[2048,4096]{1,0:T(8,128)(2,1)} fusion(bf16[2048,4096]{1,0:T(8,128)(2,1)} %reshape.124, bf16[2048]{0:T(1024)(128)(2,1)S(1)} %convert_element_type.38), kind=kLoop, calls=%fused_computation.6 | loop fusion | flops 8388608 | bytes 33558528 | tf_op jit(solution)/shard_map/mul | solution.py:89
  138.3 11.8 %gather_fusion = bf16[256,4096]{1,0:T(8,128)(2,1)S(1)} fusion(bf16[2048,4096]{1,0:T(8,128)(2,1)} %broadcast_multiply_fusion.1, s32[1024]{0:T(1024)S(1)} %pad_clamp_fusion), kind=kCustom, calls=%fused_computation | custom fusion | bytes 4195328 | tf_op jit(solution)/shard_map/jit(_take)/gather | solution.py:90
  150.2 0.3 broadcast_select_fusion
  150.4 56.4 %all_to_all.10 = bf16[8,32,4096]{2,1,0:T(8,128)(2,1)S(1)} all-to-all(bf16[8,32,4096]{2,1,0:T(8,128)(2,1)S(1)} %broadcast_select_fusion), channel_id=1, replica_groups=mesh['row'=2,'col'=4,'gz'=4] {'row','col'}, dimensions={0} | all-to-all | bytes 4194304 | tf_op jit(solution)/shard_map/all_to_all | solution.py:94
  206.8 5.5 reshape.125
  212.3 7.9 copy.19
  220.3 5.5 reshape.126
  225.8 1.3 multiply_reduce_fusion
  227.2 0.6 collective-permute-start
  227.8 1.5 collective-permute-start.1
  229.3 1.6 collective-permute-done
  230.9 0.6 collective-permute-done.1
  231.4 0.2 collective-permute-start.2
  231.6 1.9 collective-permute-start.3
  233.5 1.6 collective-permute-done.2
  235.1 1.9 collective-permute-done.3
  237.1 0.5 collective-permute-start.5
  237.6 1.1 collective-permute-done.4
  238.7 2.1 collective-permute-done.5
  241.0 1.5 collective-permute-start.6
  242.4 0.6 collective-permute-start.7
  243.1 1.7 collective-permute-done.6
  244.7 1.4 collective-permute-done.7
  246.2 0.2 collective-permute-start.8
  246.4 3.7 collective-permute-start.9
  250.0 1.6 collective-permute-done.8
  251.8 1.7 collective-permute-start.11
  253.6 2.3 collective-permute-done.10
  256.2 0.2 multiply_convert_fusion
  256.4 2.4 convolution_bitcast_fusion
  258.7 4.2 copy.20
  263.0 8.0 reshape_reshape.4
  270.9 5.2 all-to-all-start.1
  276.1 0.2 reduce-scatter.3.cloned.1.call-start
  276.5 95.1 %all-to-all-done.1 = f32[8,32,4096]{2,1,0:T(8,128)} async-done(((f32[8,32,4096]{2,1,0:T(8,128)}), f32[8,32,4096]{2,1,0:T(8,128)}, u32[]{:S(2)}, u32[]{:S(2)}) %all-to-all-start.1) | async-done | bytes 4194336 | tf_op jit(solution)/shard_map/all_to_all | solution.py:115
  371.6 20.9 %scatter_custom_fusion = f32[2048,4096]{1,0:T(8,128)} fusion(s32[256]{0:T(256)S(1)} %bitcast.67, f32[256,4096]{1,0:T(8,128)} %bitcast.21, f32[]{:T(128)} %constant.99.clone.1), kind=kCustom, calls=%fused_computation.4 | custom fusion | flops 1048576 | bytes 33554944 | tf_op jit(solution)/shard_map/scatter-add | solution.py:117
  392.5 23.3 %broadcast_multiply_fusion = f32[2048,4096]{1,0:T(8,128)} fusion(f32[2048,4096]{1,0:T(8,128)} %scatter_custom_fusion, f32[2048]{0:T(1024)S(1)} %convert_element_type.42), kind=kLoop, calls=%fused_computation.3 | loop fusion | flops 8388608 | bytes 67117056 | tf_op jit(solution)/shard_map/mul | solution.py:118
  415.8 52.6 %reshape.129 = f32[64,32,64,64]{3,2,1,0:T(8,128)} reshape(f32[2048,4096]{1,0:T(8,128)} %broadcast_multiply_fusion) | data formatting | bytes 67108864 | tf_op jit(solution)/shard_map/reshape | solution.py:119
  468.4 56.3 %copy.22 = f32[64,64,32,64]{3,2,1,0:T(8,128)} copy(f32[64,64,32,64]{3,1,2,0:T(8,128)} %bitcast.22) | data formatting | bytes 67108864 | tf_op jit(solution)/shard_map/transpose | solution.py:120
  524.8 56.5 %reshape.130 = f32[4096,2048]{1,0:T(8,128)} reshape(f32[64,64,32,64]{3,2,1,0:T(8,128)} %copy.22) | data formatting | bytes 67108864 | tf_op jit(solution)/shard_map/reshape | solution.py:120
  581.3 231.7 %reduce-scatter.3.cloned.1.call-done = f32[4096,512]{1,0:T(8,128)} async-done(((f32[4096,2048]{1,0:T(8,128)}), f32[4096,512]{1,0:T(8,128)}) %reduce-scatter.3.cloned.1.call-update) | async-done | bytes 8388624 | tf_op jit(solution)/shard_map/reduce_scatter | solution.py:121
  813.0 10.1 %fusion.19 = f32[4096,128]{1,0:T(8,128)} fusion(f32[4096,512]{1,0:T(8,128)} %reduce-scatter.3.cloned.1.call-done, f32[512,128]{1,0:T(8,128)S(1)} %copy-done), kind=kOutput, calls=%fused_computation.79 | convolution fusion | flops 3221225472 | bytes 10747904 | tf_op jit(solution)/shard_map/dot_general | solution.py:122
  823.1 61.7 %reduce-scatter.5.cloned.1.call-done = f32[256,128]{1,0:T(8,128)} async-done(((f32[4096,128]{1,0:T(8,128)}), f32[256,128]{1,0:T(8,128)}) %reduce-scatter.5.cloned.1.call-update) | async-done | bytes 131088 | tf_op jit(solution)/shard_map/reduce_scatter | solution.py:125
  (42 shorter events, 1.7 us)
Async XLA Ops:
  7.2 805.8 %copy-start = (f32[512,128]{1,0:T(8,128)S(1)}, f32[512,128]{1,0:T(8,128)}, u32[]{:S(2)}) copy-start(f32[512,128]{1,0:T(8,128)} %param.11) | copy-start | bytes 786436
  212.3 13.4 %copy-start.1 = (bf16[1,1,1,1024,384]{4,3,2,1,0:T(8,128)(2,1)S(1)}, bf16[1,1,1,1024,384]{4,3,2,1,0:T(8,128)(2,1)}, u32[]{:S(2)}) copy-start(bf16[1,1,1,1024,384]{4,3,2,1,0:T(8,128)(2,1)} %param.9) | copy-start | bytes 2359300
  220.3 6.9 copy-start.2
  227.2 3.7 collective-permute-start
  227.8 3.6 collective-permute-start.1
  231.4 3.6 collective-permute-start.2
  231.6 5.4 collective-permute-start.3
  237.1 1.6 collective-permute-start.4
  237.1 3.7 collective-permute-start.5
  241.0 3.8 collective-permute-start.6
  242.4 3.7 collective-permute-start.7
  246.2 5.5 collective-permute-start.8
  246.4 5.3 collective-permute-start.9
  251.8 4.1 collective-permute-start.10
  251.8 4.0 collective-permute-start.11
  270.9 100.7 %all-to-all-start.1 = ((f32[8,32,4096]{2,1,0:T(8,128)}), f32[8,32,4096]{2,1,0:T(8,128)}, u32[]{:S(2)}, u32[]{:S(2)}) async-start(f32[8,32,4096]{2,1,0:T(8,128)} %reshape_reshape.4), calls=%async_computation.1 | async-start | bytes 8388608 | tf_op jit(solution)/shard_map/all_to_all | solution.py:115
  276.1 536.9 %reduce-scatter.3.cloned.1.call-start = ((), (), s32[]{:S(2)}) async-start(), calls=%async_computation.4 | async-start | bytes 41943040 | tf_op jit(solution)/shard_map/reduce_scatter | solution.py:121
  581.2 303.6 %reduce-scatter.5.cloned.1.call-start = ((), (), s32[]{:S(2)}) async-start(), calls=%async_computation.5 | async-start | bytes 2228224 | tf_op jit(solution)/shard_map/reduce_scatter | solution.py:125
Sparse Core Ops, SparseCore 0:
  581.4 231.6 reduce-scatter.2
  823.2 61.5 reduce-scatter.4
where the time goes:
time: 905 us; the launch traced here: 892 us
  waiting for transfers between devices  404 us (45%)
  local copies, waits for them, and re-layouts  325 us (36%)
  other arithmetic  60.1 us (7%)
  blocking collectives  56.4 us (6%)
  starting transfers between devices  17.9 us (2%)
  between operations  14.7 us (2%)
  matrix products  13.7 us (2%)
    reduce_scatter x1, waiting for transfers between devices, shards(): share = lax.psum_scatter(dense, 'gz', scatter_dimension=1, tiled=True)  232 us
    all_to_all x1, waiting for transfers between devices, shards(): lax.all_to_all(flat_back, ('row', 'col'), split_axis=0, concat_axis=0, ti...  95.1 us
    reshape x2, local copies, waits for them, and re-layouts, shards(): density_matrix.reshape(row_blocks, block_size, column_blocks, block_size)  70.8 us
    reduce_scatter x1, waiting for transfers between devices, shards(): lax.psum_scatter(terms, ('col', 'gz'), scatter_dimension=0, tiled=True)  61.7 us
    reshape x1, local copies, waits for them, and re-layouts, shards(): dense.transpose(0, 2, 1, 3)  56.5 us
    all_to_all x1, blocking collectives, shards(): lax.all_to_all(flat_out, ('row', 'col'), split_axis=0, concat_axis=0, til...  56.4 us
    transpose x1, local copies, waits for them, and re-layouts, shards(): dense.transpose(0, 2, 1, 3)  56.3 us
    reshape x1, local copies, waits for them, and re-layouts, shards(): dense = owned.reshape(row_blocks, column_blocks, block_size, block_size)  52.6 us
  transfers between devices with their start and end apart: 15, of which 13 were waited for; matrix products, arithmetic and copies ran while one was open for 0% of the time, Pallas kernels for 0%

commit v1 on v0

--- a/solution.py
+++ b/solution.py
@@ -1,6 +1,8 @@
 import jax
 import jax.numpy as jnp
 from jax import lax
+from jax.experimental import pallas as pl
+from jax.experimental.pallas import tpu as pltpu
 from jax.sharding import PartitionSpec as P
 
 pbe_kappa = 0.804
@@ -58,7 +60,7 @@
     return first - divergence
 
 
-def shards(density_matrix, block_pattern, tile_lists, basis_values, core_density, orbitals):
+def exchanged(density_matrix, block_pattern, tile_lists, basis_values, core_density, orbitals):
     row_count = lax.axis_size("row")
     column_count = lax.axis_size("col")
     depth_count = lax.axis_size("gz")
@@ -126,6 +128,265 @@
     return (share, applied)
 
 
+vmem_bytes = 56 * 1024 * 1024
+gathered_limit = 48 * 1024 * 1024
+
+
+def density_kernel(per_row, per_column, size, rows_ref, cols_ref, keep_ref, place_ref, *refs):
+    strips = refs[:per_row]
+    phi_rows, phi_cols, out, picked, padded = refs[per_row:]
+    tile = pl.program_id(0)
+    pair_width = 2 * size
+    for n in range(per_column):
+        column = cols_ref[tile, n]
+        start = pl.multiple_of((column // 2) * pair_width, pair_width)
+        odd = column % 2
+        values = phi_cols[0, n * size : (n + 1) * size, :]
+        for half in range(2):
+            padded[n * pair_width + half * size : n * pair_width + (half + 1) * size, :] = (
+                jnp.where(odd == half, values, jnp.zeros_like(values))
+            )
+        for m in range(per_row):
+            block = strips[m][:, pl.ds(start, pair_width)]
+            kept = keep_ref[tile, m * per_column + n] != 0
+            picked[m * size : (m + 1) * size, n * pair_width : (n + 1) * pair_width] = jnp.where(
+                kept, block, jnp.zeros_like(block)
+            )
+    product = jnp.dot(picked[...], padded[...], preferred_element_type=jnp.float32)
+    rho = jnp.sum(phi_rows[0].astype(jnp.float32) * product, axis=0, keepdims=True)
+    out[0] = rho
+
+
+def partial_density(density_matrix, slab_phi, rows, cols, keep, place, size):
+    tiles, width, cells = slab_phi.shape
+    per_row, per_column = rows.shape[1], cols.shape[1]
+    columns = density_matrix.shape[1]
+
+    def strip_spec(m):
+        return pl.BlockSpec((size, columns), lambda t, rows, cols, keep, place: (rows[t, m], 0))
+
+    grid_spec = pltpu.PrefetchScalarGridSpec(
+        num_scalar_prefetch=4,
+        grid=(tiles,),
+        in_specs=[strip_spec(m) for m in range(per_row)]
+        + [
+            pl.BlockSpec(
+                (1, per_row * size, cells), lambda t, rows, cols, keep, place: (t, place[0], 0)
+            ),
+            pl.BlockSpec(
+                (1, per_column * size, cells), lambda t, rows, cols, keep, place: (t, place[1], 0)
+            ),
+        ],
+        out_specs=pl.BlockSpec((1, 1, cells), lambda t, rows, cols, keep, place: (t, 0, 0)),
+        scratch_shapes=[
+            pltpu.VMEM((per_row * size, 2 * per_column * size), jnp.bfloat16),
+            pltpu.VMEM((2 * per_column * size, cells), jnp.bfloat16),
+        ],
+    )
+
+    def body(*refs):
+        density_kernel(per_row, per_column, size, *refs)
+
+    return pl.pallas_call(
+        body,
+        grid_spec=grid_spec,
+        out_shape=jax.ShapeDtypeStruct((tiles, 1, cells), jnp.float32),
+        compiler_params=pltpu.CompilerParams(vmem_limit_bytes=vmem_bytes),
+        cost_estimate=pl.CostEstimate(
+            flops=4 * tiles * per_row * per_column * size * size * cells,
+            bytes_accessed=tiles * per_row * size * columns * 2,
+            transcendentals=0,
+        ),
+        name="partial_density",
+    )(rows, cols, keep, place, *([density_matrix] * per_row), slab_phi, slab_phi)
+
+
+def hamiltonian_kernel(
+    per_row, size, owned, rows_ref, from_ref, place_ref, phi_rows, phi_cols, field, keep, orbitals,
+    out, terms, total, weighted, padded,
+):
+    tile = pl.program_id(0)
+    pair_width = 2 * size
+
+    @pl.when(tile == 0)
+    def _():
+        total[...] = jnp.zeros_like(total)
+
+    weighted[...] = (phi_rows[0].astype(jnp.float32) * field[0]).astype(jnp.bfloat16)
+    for pair in range(owned // 2):
+        left = from_ref[tile, 2 * pair]
+        right = from_ref[tile, 2 * pair + 1]
+
+        @pl.when(jnp.maximum(left, right) >= 0)
+        def _():
+            for half, source in enumerate((left, right)):
+                start = pl.multiple_of(jnp.maximum(source, 0) * size, size)
+                values = phi_cols[0, pl.ds(start, size), :]
+                padded[half * size : (half + 1) * size, :] = jnp.where(
+                    source >= 0, values, jnp.zeros_like(values)
+                )
+            product = lax.dot_general(
+                weighted[...],
+                padded[...],
+                (((1,), (1,)), ((), ())),
+                preferred_element_type=jnp.float32,
+            )
+            span = slice(pair * pair_width, (pair + 1) * pair_width)
+            for m in range(per_row):
+                start = pl.multiple_of(rows_ref[tile, m] * size, size)
+                total[pl.ds(start, size), span] += product[m * size : (m + 1) * size]
+
+    @pl.when(tile == pl.num_programs(0) - 1)
+    def _():
+        step = 4 * size
+
+        @pl.loop(0, total.shape[0] // step)
+        def _(chunk):
+            for part in range(4):
+                span = pl.ds(pl.multiple_of(chunk * step + part * size, size), size)
+                out[span, :] = total[span, :] * keep[pl.ds(chunk * 4 + part, 1), :]
+            span = pl.ds(pl.multiple_of(chunk * step, step), step)
+            terms[span, :] = jnp.dot(
+                out[span, :],
+                orbitals[...],
+                precision=lax.Precision.HIGHEST,
+                preferred_element_type=jnp.float32,
+            )
+
+
+def owned_hamiltonian(phi, field, rows, sources, place, keep, orbitals, size, per_column):
+    tiles, width, cells = phi.shape
+    per_row = rows.shape[1]
+    owned = sources.shape[1]
+    high = keep.shape[0] * size
+    wide = owned * size
+    norb = orbitals.shape[1]
+    grid_spec = pltpu.PrefetchScalarGridSpec(
+        num_scalar_prefetch=3,
+        grid=(tiles,),
+        in_specs=[
+            pl.BlockSpec((1, per_row * size, cells), lambda t, rows, sources, place: (t, place[0], 0)),
+            pl.BlockSpec(
+                (1, per_column * size, cells), lambda t, rows, sources, place: (t, place[1], 0)
+            ),
+            pl.BlockSpec((1, 1, cells), lambda t, rows, sources, place: (t, 0, 0)),
+            pl.BlockSpec(keep.shape, lambda t, rows, sources, place: (0, 0)),
+            pl.BlockSpec(orbitals.shape, lambda t, rows, sources, place: (0, 0)),
+        ],
+        out_specs=[
+            pl.BlockSpec((high, wide), lambda t, rows, sources, place: (0, 0)),
+            pl.BlockSpec((high, norb), lambda t, rows, sources, place: (0, 0)),
+        ],
+        scratch_shapes=[
+            pltpu.VMEM((high, wide), jnp.float32),
+            pltpu.VMEM((per_row * size, cells), jnp.bfloat16),
+            pltpu.VMEM((2 * size, cells), jnp.bfloat16),
+        ],
+    )
+
+    def body(*refs):
+        hamiltonian_kernel(per_row, size, owned, *refs)
+
+    return pl.pallas_call(
+        body,
+        grid_spec=grid_spec,
+        out_shape=[
+            jax.ShapeDtypeStruct((high, wide), jnp.float32),
+            jax.ShapeDtypeStruct((high, norb), jnp.float32),
+        ],
+        compiler_params=pltpu.CompilerParams(vmem_limit_bytes=vmem_bytes),
+        name="owned_hamiltonian",
+    )(rows, sources, place, phi, phi, field, keep, orbitals)
+
+
+def whole_potential(density):
+    def difference(values, direction):
+        return (jnp.roll(values, -1, direction) - jnp.roll(values, 1, direction)) / (2.0 * spacing)
+
+    gradients = [difference(density, direction) for direction in range(3)]
+    grad_square = (
+        gradients[0] * gradients[0] + gradients[1] * gradients[1] + gradients[2] * gradients[2]
+    )
+    first, second = jax.grad(total_energy, argnums=(0, 1))(density, grad_square)
+    divergence = sum(
+        difference(2.0 * second * gradients[direction], direction) for direction in range(3)
+    )
+    return first - divergence
+
+
+def gathered(density_matrix, block_pattern, tile_lists, basis_values, core_density, orbitals):
+    row_count = lax.axis_size("row")
+    column_count = lax.axis_size("col")
+    depth_count = lax.axis_size("gz")
+    row_index = lax.axis_index("row")
+    column_index = lax.axis_index("col")
+    depth_index = lax.axis_index("gz")
+    row_blocks, column_blocks = block_pattern.shape
+    size = density_matrix.shape[0] // row_blocks
+    tiles, listed = tile_lists.shape
+    per_row = listed // row_count
+    per_column = listed // column_count
+    owned = column_blocks // depth_count
+    cells = core_density.size
+    phi_tile = basis_values.reshape(listed * size, cells)
+
+    lists = tile_lists.reshape(row_count, column_count, depth_count, listed).transpose(2, 0, 1, 3)
+    lists = lists.reshape(tiles, listed)
+    rows = lax.dynamic_slice_in_dim(lists, row_index * per_row, per_row, 1) - row_index * row_blocks
+    cols = (
+        lax.dynamic_slice_in_dim(lists, column_index * per_column, per_column, 1)
+        - column_index * column_blocks
+    )
+    slab = row_count * column_count
+    slab_rows = lax.dynamic_slice_in_dim(rows, depth_index * slab, slab, 0)
+    slab_cols = lax.dynamic_slice_in_dim(cols, depth_index * slab, slab, 0)
+    slab_keep = block_pattern[slab_rows[:, :, None], slab_cols[:, None, :]]
+    slab_keep = slab_keep.reshape(slab, per_row * per_column)
+    place = jnp.stack([row_index, column_index]).astype(jnp.int32)
+    own_ids = depth_index * owned + jnp.arange(owned, dtype=jnp.int32)
+    matches = cols[:, None, :] == own_ids[None, :, None]
+    numbers = jnp.arange(per_column, dtype=jnp.int32)[None, None, :]
+    sources = jnp.max(jnp.where(matches, numbers, -1), axis=2).astype(jnp.int32)
+    own_pattern = lax.dynamic_slice_in_dim(block_pattern, depth_index * owned, owned, 1)
+    keep = jnp.repeat(own_pattern.astype(jnp.float32), size, axis=1)
+
+    slab_phi = lax.all_gather(phi_tile, ("row", "col"), axis=0, tiled=False)
+    slab_phi = slab_phi.reshape(slab, listed * size, cells)
+    phi = lax.all_gather(slab_phi, "gz", axis=0, tiled=True)
+
+    partial = partial_density(
+        density_matrix, slab_phi, slab_rows, slab_cols, slab_keep, place, size
+    )
+    partial = partial.reshape(slab, cells)
+    own_tile = (row_index * column_count + column_index) == jnp.arange(slab)[:, None]
+    partial = partial + jnp.where(own_tile, core_density.reshape(1, cells), 0.0)
+    parts = lax.all_gather(partial, ("row", "col", "gz"), axis=0, tiled=False)
+    parts = parts.reshape(slab, depth_count, slab, cells).sum(axis=0)
+    tile_shape = core_density.shape
+    grid = parts.reshape((depth_count, row_count, column_count) + tile_shape)
+    grid = grid.transpose(1, 3, 2, 4, 0, 5).reshape(
+        row_count * tile_shape[0], column_count * tile_shape[1], depth_count * tile_shape[2]
+    )
+    field = whole_potential(jnp.maximum(grid, density_floor))
+    field = field.reshape(
+        row_count, tile_shape[0], column_count, tile_shape[1], depth_count, tile_shape[2]
+    )
+    field = field.transpose(4, 0, 2, 1, 3, 5).reshape(tiles, 1, cells)
+    hamiltonian, terms = owned_hamiltonian(
+        phi, field, rows, sources, place, keep, orbitals, size, per_column
+    )
+    applied = lax.psum_scatter(terms, ("col", "gz"), scatter_dimension=0, tiled=True)
+    return hamiltonian, applied
+
+
+def shards(density_matrix, block_pattern, tile_lists, basis_values, core_density, orbitals):
+    arguments = (
+        density_matrix, block_pattern, tile_lists, basis_values, core_density, orbitals,
+    )
+    fits = tile_lists.shape[0] * basis_values.size * 2 <= gathered_limit
+    return gathered(*arguments) if fits else exchanged(*arguments)
+
+
 def solution(mesh):
     placed = (
         P("row", "col"),

time: 905 us -> 383 us (0.42); the launches traced: 892 us -> 381 us
  local copies, waits for them, and re-layouts: 325 us -> 8.84 us
  waiting for transfers between devices: 404 us -> 258 us
  other arithmetic: 60.1 us -> 4.29 us
  Pallas kernels: 0 us -> 55.2 us
  starting transfers between devices: 17.9 us -> 0.11 us
  blocking collectives: 56.4 us -> 40.5 us
  matrix products: 13.7 us -> 0 us
    reshape x8 -> x3, local copies, waits for them, and re-layouts: 235 us -> 2.27 us  [the longest x1 0.82 us: gathered(): field = field.transpose(4, 0, 2, 1, 3, 5).reshape(tiles, 1, cells)]
    reduce_scatter x2 -> x1, waiting for transfers between devices: 293 us -> 63.8 us  [gathered(): lax.psum_scatter(terms, ('col', 'gz'), scatter_dimension=0, tiled=True)]
    all_gather x0 -> x2, waiting for transfers between devices: none -> 194 us  [the longest x1 104 us: gathered(): slab_phi = lax.all_gather(phi_tile, ('row', 'col'), axis=0, tiled=False)]
    all_to_all x1 -> x0, waiting for transfers between devices: 95.1 us -> none  [shards(): lax.all_to_all(flat_back, ('row', 'col'), split_axis=0, concat_axis=0, ti...]
    transpose x3 -> x2, local copies, waits for them, and re-layouts: 68.5 us -> 0.03 us  [the longest x1 0.02 us: gathered(): field = field.transpose(4, 0, 2, 1, 3, 5).reshape(tiles, 1, cells)]
    all_to_all x1 -> x0, blocking collectives: 56.4 us -> none  [shards(): lax.all_to_all(flat_out, ('row', 'col'), split_axis=0, concat_axis=0, til...]
    pallas_call x0 -> x2, Pallas kernels: none -> 55.2 us  [the longest x1 40.5 us: owned_hamiltonian(): pl.pallas_call(body, grid_spec=grid_spec, out_shape=[jax.ShapeDtypeStruct...]
    all_gather x0 -> x1, blocking collectives: none -> 40.5 us  [gathered(): parts = lax.all_gather(partial, ('row', 'col', 'gz'), axis=0, tiled=False)]
  transfers between devices with their start and end apart: 15 -> 3, of which waited for: 13 -> 3; matrix products, arithmetic and copies ran while one was open for 0% -> 3% of each run, Pallas kernels for 0% -> 4%
where the time goes in v1:
time: 383 us; the launch traced here: 381 us
  waiting for transfers between devices  258 us (67%)
  Pallas kernels  55.2 us (14%)
  blocking collectives  40.5 us (11%)
  between operations  14 us (4%)
  local copies, waits for them, and re-layouts  8.84 us (2%)
  other arithmetic  4.29 us (1%)
    all_gather x1, waiting for transfers between devices, gathered(): slab_phi = lax.all_gather(phi_tile, ('row', 'col'), axis=0, tiled=False)  104 us
    all_gather x1, waiting for transfers between devices, gathered(): phi = lax.all_gather(slab_phi, 'gz', axis=0, tiled=True)  89.9 us
    reduce_scatter x1, waiting for transfers between devices, gathered(): lax.psum_scatter(terms, ('col', 'gz'), scatter_dimension=0, tiled=True)  63.8 us
    pallas_call x1, Pallas kernels, owned_hamiltonian(): pl.pallas_call(body, grid_spec=grid_spec, out_shape=[jax.ShapeDtypeStruct...  40.5 us
    all_gather x1, blocking collectives, gathered(): parts = lax.all_gather(partial, ('row', 'col', 'gz'), axis=0, tiled=False)  40.5 us
    pallas_call x1, Pallas kernels, partial_density(): pl.pallas_call(body, grid_spec=grid_spec, out_shape=jax.ShapeDtypeStruct(...  14.7 us
  transfers between devices with their start and end apart: 3, of which 3 were waited for; matrix products, arithmetic and copies ran while one was open for 3% of the time, Pallas kernels for 4%

profile of v1, /device:TPU:0, one launch (start us, length us, event | category | flops | bytes accessed | tf_op | source)
XLA Modules:
  0.0 381.3 jit_solution(2805373629174458815)
XLA Ops:
  7.2 0.0 all-gather.5.cloned.1.call-start
  7.2 0.7 all-gather.5.cloned.1.call-update
  7.9 0.0 all-gather.7.cloned.1.call-start
  8.0 103.9 %all-gather.5.cloned.1.call-done = bf16[8,1,1,1024,384]{4,3,2,1,0:T(8,128)(2,1)} async-done(((bf16[1,1,1,1024,384]{4,3,2,1,0:T(8,128)(2,1)}), bf16[8,1,1,1024,384]{4,3,2,1,0:T(8,128)(2,1)}) %all-gather.5.cloned.1.call-update) | async-done | bytes 6291472 | tf_op jit(solution)/shard_map/all_gather | solution.py:353
  111.9 0.0 all-gather.7.cloned.1.call-update
  111.9 0.0 reduce-scatter.2.cloned.1.call-start
  111.9 0.8 broadcast_in_dim.58
  112.7 0.8 copy.60
  113.5 0.1 dynamic-slice_subtract_fusion
  113.6 0.1 copy.62
  113.7 0.1 select_reduce_fusion
  113.8 0.7 copy.73.refs_1_
  114.4 0.6 fusion.14
  115.0 0.1 dynamic-slice_subtract_fusion.1.refs_0_
  115.1 0.6 fusion.12
  115.7 0.1 broadcast_or_fusion
  115.8 0.1 reshape.172
  115.9 2.0 gather_fusion
  117.9 0.7 reshape.157.refs_2_
  118.6 0.1 copy.72
  118.7 0.1 broadcast_in_dim.61
  118.8 0.8 reshape.161.refs_6_
  119.6 0.6 pad_add_fusion.refs_3_.refs_2_
  120.2 14.7 %partial_density.1 = f32[8,1,384]{2,1,0:T(1,128)} custom-call(s32[8,8]{1,0:T(8,128)} %get-tuple-element.10.refs_0_, s32[8,4]{1,0:T(8,128)} %get-tuple-element.12.refs_1_, s32[8,32]{1,0:T(8,128)} %reshape.157.refs_2_, s32[2]{0:T(128)} %pad_add_fusion.refs_3_.refs_2_, bf16[4096,2048]{1,0:T(8,128)(2,1)} %refs_11_.1, bf16[4096,2048]{1,0:T(8,128)(2,1)} %refs_11_.1, ...), custom_call_target="tpu_custom_call" | custom-call | flops 1610612736 | bytes 16777216 | tf_op jit(solution)/shard_map/partial_density/pallas_call | solution.py:190
  134.9 0.8 fusion.10
  135.7 40.5 %all_gather.12 = f32[32,8,384]{2,1,0:T(8,128)S(1)} all-gather(f32[1,8,384]{2,1,0:T(8,128)S(1)} %copy.63), channel_id=1, replica_groups=mesh['row'=2,'col'=4,'gz'=4] {'row','col','gz'}, dimensions={0}, use_global_device_ids=true | all-gather | bytes 405504 | tf_op jit(solution)/shard_map/all_gather | solution.py:363
  176.2 0.1 power_multiply_fusion.2
  176.4 0.2 reshape.164
  176.5 0.2 reshape.166
  176.7 0.2 reshape.171
  176.9 0.2 reshape.170
  177.1 0.2 max.20
  177.3 0.2 copy.66
  177.4 0.2 max.22
  177.7 0.1 fusion.29
  177.7 0.1 fusion.28
  177.8 0.2 fusion.17
  178.2 0.1 fusion.19
  178.2 0.1 fusion.18
  178.3 0.1 fusion.9
  178.4 0.2 add.102
  178.6 0.2 reshape.162
  178.8 0.9 fusion.3
  179.7 0.8 reshape.160.refs_5_
  180.5 89.9 %all-gather.7.cloned.1.call-done = bf16[32,1,1,1024,384]{4,3,2,1,0:T(8,128)(2,1)} async-done(((bf16[8,1,1,1024,384]{4,3,2,1,0:T(8,128)(2,1)}), bf16[32,1,1,1024,384]{4,3,2,1,0:T(8,128)(2,1)}) %all-gather.7.cloned.1.call-update) | async-done | bytes 25165840 | tf_op jit(solution)/shard_map/all_gather | solution.py:355
  270.4 40.5 %owned_hamiltonian.1 = (f32[4096,512]{1,0:T(8,128)}, f32[4096,128]{1,0:T(8,128)}) custom-call(s32[32,8]{1,0:T(8,128)} %copy-done.1, s32[32,8]{1,0:T(8,128)} %copy.73.refs_1_, s32[2]{0:T(128)} %pad_add_fusion.refs_3_.refs_2_, bf16[32,1024,384]{2,1,0:T(8,128)(2,1)} %bitcast.45, bf16[32,1024,384]{2,1,0:T(8,128)(2,1)} %bitcast.46, ...), custom_call_target="tpu_custom_call" | custom-call | tf_op jit(solution)/shard_map/owned_hamiltonian/pallas_call | solution.py:290
  311.0 0.0 reduce-scatter.2.cloned.1.call-update
  311.0 63.8 %reduce-scatter.2.cloned.1.call-done = f32[256,128]{1,0:T(8,128)} async-done(((f32[4096,128]{1,0:T(8,128)}), f32[256,128]{1,0:T(8,128)}) %reduce-scatter.2.cloned.1.call-update) | async-done | bytes 131088 | tf_op jit(solution)/shard_map/reduce_scatter | solution.py:378
  (20 shorter events, 0.2 us)
Async XLA Ops:
  7.2 108.7 %copy-start = (s32[64,32]{0,1:T(8,128)S(1)}, s32[64,32]{0,1:T(8,128)}, u32[]{:S(2)}) copy-start(s32[64,32]{0,1:T(8,128)} %param.7) | copy-start | bytes 24580
  7.2 104.7 %all-gather.5.cloned.1.call-start = ((), (), s32[]{:S(2)}) async-start(), calls=%async_computation.2 | async-start | bytes 7077888 | tf_op jit(solution)/shard_map/all_gather | solution.py:353
  7.9 262.5 %all-gather.7.cloned.1.call-start = ((), (), s32[]{:S(2)}) async-start(), calls=%async_computation.3 | async-start | bytes 31457280 | tf_op jit(solution)/shard_map/all_gather | solution.py:355
  111.9 262.9 %reduce-scatter.2.cloned.1.call-start = ((), (), s32[]{:S(2)}) async-start(), calls=%async_computation.1 | async-start | bytes 2228224 | tf_op jit(solution)/shard_map/reduce_scatter | solution.py:378
  115.1 2.8 copy-start.1
Sparse Core Ops, SparseCore 0:
  10.1 101.7 all-gather.4
  113.4 156.9 all-gather.6
  311.1 63.6 reduce-scatter.1

commit v2 on v1

--- a/solution.py
+++ b/solution.py
@@ -132,16 +132,295 @@
 gathered_limit = 48 * 1024 * 1024
 
 
+MESH = pl.DeviceIdType.MESH
+
+
+def meet(peers):
+    barrier = pltpu.get_barrier_semaphore()
+    for peer in peers:
+        pl.semaphore_signal(barrier, inc=1, device_id=peer, device_id_type=MESH)
+    pl.semaphore_wait(barrier, len(peers))
+
+
+def basis_kernel(row_count, column_count, phi, rows_out, cols_out, own_sem, send, got, got_cols):
+    i, j, k = lax.axis_index("row"), lax.axis_index("col"), lax.axis_index("gz")
+    across = 1 - i
+    beside = lax.rem(k + 2, 4)
+    twin = k + 1 - 2 * lax.rem(k, 2)
+    half = column_count // row_count
+    share = phi.shape[1] // half
+    provider = (j // half) == i
+    offset = pl.multiple_of(lax.rem(j, half) * share, share)
+    others = [lax.rem(j + step, column_count) for step in range(1, column_count)]
+    x_peer, y_peer, c_peer = (across, j, k), (i, j, beside), (i, j, twin)
+    z_peers = [(i, other, k) for other in others]
+    meet([x_peer, y_peer, c_peer] + z_peers)
+    started, started_cols, started_twin = [], [], []
+
+    def push(source, target, arrival, peer, log):
+        number = len(started) + len(started_cols) + len(started_twin)
+        copy = pltpu.make_async_remote_copy(
+            src_ref=source, dst_ref=target, send_sem=send.at[number], recv_sem=arrival,
+            device_id=peer, device_id_type=MESH,
+        )
+        log.append(copy)
+        return copy
+
+    def arrived(out, sems, where):
+        pltpu.make_async_remote_copy(
+            src_ref=out.at[where], dst_ref=out.at[where], send_sem=send.at[0],
+            recv_sem=sems.at[where], device_id=x_peer, device_id_type=MESH,
+        ).wait_recv()
+
+    own = (k, i, j)
+    local = pltpu.make_async_copy(phi.at[i], rows_out.at[own], own_sem)
+    local.start()
+    push(phi.at[across], rows_out.at[own], got.at[own], x_peer, started).start()
+
+    queue = []
+
+    def spread(source, where, along_z, along_y):
+        if along_z:
+            for peer in z_peers:
+                push(source, rows_out.at[where], got.at[where], peer, started).start()
+        if along_y:
+            push(source, rows_out.at[where], got.at[where], y_peer, started).start()
+        column = push(
+            source.at[pl.ds(offset, share)], cols_out.at[where], got_cols.at[where], x_peer,
+            started_cols,
+        )
+        pl.when(provider)(column.start)
+        push(source, rows_out.at[where], got.at[where], c_peer, started).start()
+        queue.append(where)
+        if len(queue) > 3:
+            relay(queue.pop(0))
+
+    def relay(where):
+        copy = push(
+            cols_out.at[where], cols_out.at[where], got_cols.at[where], c_peer, started_twin
+        )
+
+        @pl.when(jnp.logical_not(provider))
+        def _():
+            arrived(cols_out, got_cols, where)
+            copy.start()
+
+    spread(phi.at[i], own, True, True)
+    where = (k, across, j)
+    arrived(rows_out, got, where)
+    spread(rows_out.at[where], where, True, True)
+    slab = [(side, other) for side in (i, across) for other in others]
+    for side, other in slab:
+        where = (k, side, other)
+        arrived(rows_out, got, where)
+        spread(rows_out.at[where], where, False, True)
+    for side, other in [(i, j), (across, j)] + slab:
+        where = (beside, side, other)
+        arrived(rows_out, got, where)
+        spread(rows_out.at[where], where, False, False)
+    while queue:
+        relay(queue.pop(0))
+    for depth in (twin, lax.rem(twin + 2, 4)):
+        for side, other in [(i, j), (across, j)] + slab:
+            arrived(rows_out, got, (depth, side, other))
+
+    @pl.when(jnp.logical_not(provider))
+    def _():
+        for depth in (twin, lax.rem(twin + 2, 4)):
+            for side, other in [(i, j), (across, j)] + slab:
+                arrived(cols_out, got_cols, (depth, side, other))
+        for copy in started_twin:
+            copy.wait_send()
+
+    @pl.when(provider)
+    def _():
+        for copy in started_cols:
+            copy.wait_send()
+
+    for copy in started:
+        copy.wait_send()
+    local.wait()
+
+
+def gather_basis(phi_tile, row_count, column_count, depth_count):
+    width, cells = phi_tile.shape
+    halves = phi_tile.reshape(row_count, width // row_count, cells)
+    grid = (depth_count, row_count, column_count)
+    count = row_count * column_count
+    messages = 1 + row_count * (column_count - 1) + count + 3 * 2 * count
+
+    def body(*refs):
+        basis_kernel(row_count, column_count, *refs)
+
+    rows_phi, cols_phi = pl.pallas_call(
+        body,
+        in_specs=[pl.BlockSpec(memory_space=pltpu.HBM)],
+        out_specs=[pl.BlockSpec(memory_space=pltpu.HBM)] * 2,
+        out_shape=[
+            jax.ShapeDtypeStruct(grid + (width // row_count, cells), phi_tile.dtype),
+            jax.ShapeDtypeStruct(grid + (width // column_count, cells), phi_tile.dtype),
+        ],
+        scratch_shapes=[
+            pltpu.SemaphoreType.DMA,
+            pltpu.SemaphoreType.DMA((messages,)),
+            pltpu.SemaphoreType.DMA(grid),
+            pltpu.SemaphoreType.DMA(grid),
+        ],
+        compiler_params=pltpu.CompilerParams(collective_id=0, has_side_effects=True),
+        name="gather_basis",
+    )(halves)
+    tiles = depth_count * count
+    return (
+        rows_phi.reshape(tiles, width // row_count, cells),
+        cols_phi.reshape(tiles, width // column_count, cells),
+    )
+
+
+def sum_kernel(row_count, column_count, depth_count, partial, out, slots, slabs, send, got, got_slab):
+    i, j, k = lax.axis_index("row"), lax.axis_index("col"), lax.axis_index("gz")
+    count = row_count * column_count
+    me = i * column_count + j
+    peers = [lax.rem(me + step, count) for step in range(1, count)]
+    depths = [lax.rem(k + step, depth_count) for step in range(1, depth_count)]
+    ids = [(peer // column_count, lax.rem(peer, column_count), k) for peer in peers]
+    depth_ids = [(i, j, depth) for depth in depths]
+    meet(ids + depth_ids)
+    copies = []
+    for number, peer in enumerate(ids):
+        copy = pltpu.make_async_remote_copy(
+            src_ref=partial, dst_ref=slots.at[me], send_sem=send.at[number],
+            recv_sem=got.at[me], device_id=peer, device_id_type=MESH,
+        )
+        copy.start()
+        copies.append(copy)
+    slots[me] = partial[...]
+    for peer in peers:
+        pltpu.make_async_remote_copy(
+            src_ref=partial, dst_ref=slots.at[peer], send_sem=send.at[0],
+            recv_sem=got.at[peer], device_id=ids[0], device_id_type=MESH,
+        ).wait_recv()
+    summed = slots[0]
+    for number in range(1, count):
+        summed = summed + slots[number]
+    slabs[k] = summed
+    for number, peer in enumerate(depth_ids):
+        copy = pltpu.make_async_remote_copy(
+            src_ref=slabs.at[k], dst_ref=slabs.at[k], send_sem=send.at[count - 1 + number],
+            recv_sem=got_slab.at[k], device_id=peer, device_id_type=MESH,
+        )
+        copy.start()
+        copies.append(copy)
+    for depth in depths:
+        pltpu.make_async_remote_copy(
+            src_ref=partial, dst_ref=slabs.at[depth], send_sem=send.at[0],
+            recv_sem=got_slab.at[depth], device_id=ids[0], device_id_type=MESH,
+        ).wait_recv()
+    out[...] = slabs[...]
+    for copy in copies:
+        copy.wait_send()
+
+
+def sum_density(partial, row_count, column_count, depth_count):
+    count = row_count * column_count
+
+    def body(*refs):
+        sum_kernel(row_count, column_count, depth_count, *refs)
+
+    return pl.pallas_call(
+        body,
+        in_specs=[pl.BlockSpec(memory_space=pltpu.VMEM)],
+        out_specs=pl.BlockSpec(memory_space=pltpu.VMEM),
+        out_shape=jax.ShapeDtypeStruct((depth_count,) + partial.shape, partial.dtype),
+        scratch_shapes=[
+            pltpu.VMEM((count,) + partial.shape, partial.dtype),
+            pltpu.VMEM((depth_count,) + partial.shape, partial.dtype),
+            pltpu.SemaphoreType.DMA((count + depth_count,)),
+            pltpu.SemaphoreType.DMA((count,)),
+            pltpu.SemaphoreType.DMA((depth_count,)),
+        ],
+        compiler_params=pltpu.CompilerParams(collective_id=1, has_side_effects=True),
+        name="sum_density",
+    )(partial)
+
+
+def applied_kernel(column_count, terms, out, c_got, y_send, y_got, z_send, z_got, send, got):
+    i, j, k = lax.axis_index("row"), lax.axis_index("col"), lax.axis_index("gz")
+    y, c = k // 2, lax.rem(k, 2)
+    y_peer, c_peer = (i, j, lax.rem(k + 2, 4)), (i, j, k + 1 - 2 * c)
+    others = [lax.rem(j + step, column_count) for step in range(1, column_count)]
+    z_peers = [(i, other, k) for other in others]
+    meet([y_peer, c_peer] + z_peers)
+
+    def push(number, source, target, peer):
+        copy = pltpu.make_async_remote_copy(
+            src_ref=source, dst_ref=target, send_sem=send.at[number], recv_sem=got.at[number],
+            device_id=peer, device_id_type=MESH,
+        )
+        copy.start()
+        return copy
+
+    first = push(0, terms.at[1 - y, 1 - c], c_got.at[0], c_peer)
+    second = push(1, terms.at[y, 1 - c], c_got.at[1], c_peer)
+    first.wait_recv()
+    y_send[...] = terms[1 - y, c] + c_got[0]
+    third = push(2, y_send, y_got, y_peer)
+    second.wait_recv()
+    z_send[...] = terms[y, c] + c_got[1]
+    third.wait_recv()
+    z_send[...] = z_send[...] + y_got[...]
+    last = []
+    for number, (other, peer) in enumerate(zip(others, z_peers)):
+        last.append(push(3 + number, z_send.at[other], z_got.at[number], peer))
+    total = z_send[j]
+    for number, copy in enumerate(last):
+        copy.wait_recv()
+        total = total + z_got[number]
+    out[...] = total
+    for copy in [first, second, third] + last:
+        copy.wait_send()
+
+
+def sum_applied(terms, column_count):
+    high, norb = terms.shape
+    rows = high // (4 * column_count)
+    parts = terms.reshape(column_count, 2, 2, rows, norb).transpose(1, 2, 0, 3, 4)
+    part = (column_count, rows, norb)
+
+    def body(*refs):
+        applied_kernel(column_count, *refs)
+
+    return pl.pallas_call(
+        body,
+        in_specs=[pl.BlockSpec(memory_space=pltpu.VMEM)],
+        out_specs=pl.BlockSpec(memory_space=pltpu.VMEM),
+        out_shape=jax.ShapeDtypeStruct((rows, norb), terms.dtype),
+        scratch_shapes=[
+            pltpu.VMEM((2,) + part, terms.dtype),
+            pltpu.VMEM(part, terms.dtype),
+            pltpu.VMEM(part, terms.dtype),
+            pltpu.VMEM(part, terms.dtype),
+            pltpu.VMEM((column_count - 1, rows, norb), terms.dtype),
+            pltpu.SemaphoreType.DMA((2 + column_count,)),
+            pltpu.SemaphoreType.DMA((2 + column_count,)),
+        ],
+        compiler_params=pltpu.CompilerParams(
+            collective_id=2, has_side_effects=True, vmem_limit_bytes=vmem_bytes // 2
+        ),
+        name="sum_applied",
+    )(parts)
+
+
 def density_kernel(per_row, per_column, size, rows_ref, cols_ref, keep_ref, place_ref, *refs):
     strips = refs[:per_row]
-    phi_rows, phi_cols, out, picked, padded = refs[per_row:]
+    phi_rows, phi_near, phi_far, out, picked, padded = refs[per_row:]
     tile = pl.program_id(0)
     pair_width = 2 * size
     for n in range(per_column):
         column = cols_ref[tile, n]
         start = pl.multiple_of((column // 2) * pair_width, pair_width)
         odd = column % 2
-        values = phi_cols[0, n * size : (n + 1) * size, :]
+        span = slice(n * size, (n + 1) * size)
+        values = jnp.where(place_ref[1] == 1, phi_near[0, span, :], phi_far[0, span, :])
         for half in range(2):
             padded[n * pair_width + half * size : n * pair_width + (half + 1) * size, :] = (
                 jnp.where(odd == half, values, jnp.zeros_like(values))
@@ -157,8 +436,8 @@
     out[0] = rho
 
 
-def partial_density(density_matrix, slab_phi, rows, cols, keep, place, size):
-    tiles, width, cells = slab_phi.shape
+def partial_density(density_matrix, rows_phi, cols_phi, rows, cols, keep, place, size):
+    tiles, cells = rows.shape[0], rows_phi.shape[2]
     per_row, per_column = rows.shape[1], cols.shape[1]
     columns = density_matrix.shape[1]
 
@@ -171,10 +450,16 @@
         in_specs=[strip_spec(m) for m in range(per_row)]
         + [
             pl.BlockSpec(
-                (1, per_row * size, cells), lambda t, rows, cols, keep, place: (t, place[0], 0)
+                (1, per_row * size, cells),
+                lambda t, rows, cols, keep, place: (place[2] + t, 0, 0),
             ),
             pl.BlockSpec(
-                (1, per_column * size, cells), lambda t, rows, cols, keep, place: (t, place[1], 0)
+                (1, per_column * size, cells),
+                lambda t, rows, cols, keep, place: ((place[2] + t) * place[1], place[0], 0),
+            ),
+            pl.BlockSpec(
+                (1, per_column * size, cells),
+                lambda t, rows, cols, keep, place: ((place[2] + t) * (1 - place[1]), 0, 0),
             ),
         ],
         out_specs=pl.BlockSpec((1, 1, cells), lambda t, rows, cols, keep, place: (t, 0, 0)),
@@ -198,11 +483,11 @@
             transcendentals=0,
         ),
         name="partial_density",
-    )(rows, cols, keep, place, *([density_matrix] * per_row), slab_phi, slab_phi)
+    )(rows, cols, keep, place, *([density_matrix] * per_row), rows_phi, rows_phi, cols_phi)
 
 
 def hamiltonian_kernel(
-    per_row, size, owned, rows_ref, from_ref, place_ref, phi_rows, phi_cols, field, keep, orbitals,
+    per_row, size, owned, rows_ref, from_ref, place_ref, phi_rows, phi_near, phi_far, field, keep, orbitals,
     out, terms, total, weighted, padded,
 ):
     tile = pl.program_id(0)
@@ -221,7 +506,8 @@
         def _():
             for half, source in enumerate((left, right)):
                 start = pl.multiple_of(jnp.maximum(source, 0) * size, size)
-                values = phi_cols[0, pl.ds(start, size), :]
+                span = pl.ds(start, size)
+                values = jnp.where(place_ref[1] == 1, phi_near[0, span, :], phi_far[0, span, :])
                 padded[half * size : (half + 1) * size, :] = jnp.where(
                     source >= 0, values, jnp.zeros_like(values)
                 )
@@ -254,8 +540,8 @@
             )
 
 
-def owned_hamiltonian(phi, field, rows, sources, place, keep, orbitals, size, per_column):
-    tiles, width, cells = phi.shape
+def owned_hamiltonian(rows_phi, cols_phi, field, rows, sources, place, keep, orbitals, size, per_column):
+    tiles, width, cells = rows_phi.shape
     per_row = rows.shape[1]
     owned = sources.shape[1]
     high = keep.shape[0] * size
@@ -265,9 +551,14 @@
         num_scalar_prefetch=3,
         grid=(tiles,),
         in_specs=[
-            pl.BlockSpec((1, per_row * size, cells), lambda t, rows, sources, place: (t, place[0], 0)),
+            pl.BlockSpec((1, per_row * size, cells), lambda t, rows, sources, place: (t, 0, 0)),
             pl.BlockSpec(
-                (1, per_column * size, cells), lambda t, rows, sources, place: (t, place[1], 0)
+                (1, per_column * size, cells),
+                lambda t, rows, sources, place: (t * place[1], place[0], 0),
+            ),
+            pl.BlockSpec(
+                (1, per_column * size, cells),
+                lambda t, rows, sources, place: (t * (1 - place[1]), 0, 0),
             ),
             pl.BlockSpec((1, 1, cells), lambda t, rows, sources, place: (t, 0, 0)),
             pl.BlockSpec(keep.shape, lambda t, rows, sources, place: (0, 0)),
@@ -296,7 +587,7 @@
         ],
         compiler_params=pltpu.CompilerParams(vmem_limit_bytes=vmem_bytes),
         name="owned_hamiltonian",
-    )(rows, sources, place, phi, phi, field, keep, orbitals)
+    )(rows, sources, place, rows_phi, rows_phi, cols_phi, field, keep, orbitals)
 
 
 def whole_potential(density):
@@ -342,7 +633,9 @@
     slab_cols = lax.dynamic_slice_in_dim(cols, depth_index * slab, slab, 0)
     slab_keep = block_pattern[slab_rows[:, :, None], slab_cols[:, None, :]]
     slab_keep = slab_keep.reshape(slab, per_row * per_column)
-    place = jnp.stack([row_index, column_index]).astype(jnp.int32)
+    half = column_count // row_count
+    near = (column_index // half == row_index).astype(jnp.int32)
+    place = jnp.stack([column_index % half, near, depth_index * slab]).astype(jnp.int32)
     own_ids = depth_index * owned + jnp.arange(owned, dtype=jnp.int32)
     matches = cols[:, None, :] == own_ids[None, :, None]
     numbers = jnp.arange(per_column, dtype=jnp.int32)[None, None, :]
@@ -350,18 +643,14 @@
     own_pattern = lax.dynamic_slice_in_dim(block_pattern, depth_index * owned, owned, 1)
     keep = jnp.repeat(own_pattern.astype(jnp.float32), size, axis=1)
 
-    slab_phi = lax.all_gather(phi_tile, ("row", "col"), axis=0, tiled=False)
-    slab_phi = slab_phi.reshape(slab, listed * size, cells)
-    phi = lax.all_gather(slab_phi, "gz", axis=0, tiled=True)
-
+    rows_phi, cols_phi = gather_basis(phi_tile, row_count, column_count, depth_count)
     partial = partial_density(
-        density_matrix, slab_phi, slab_rows, slab_cols, slab_keep, place, size
+        density_matrix, rows_phi, cols_phi, slab_rows, slab_cols, slab_keep, place, size
     )
     partial = partial.reshape(slab, cells)
     own_tile = (row_index * column_count + column_index) == jnp.arange(slab)[:, None]
     partial = partial + jnp.where(own_tile, core_density.reshape(1, cells), 0.0)
-    parts = lax.all_gather(partial, ("row", "col", "gz"), axis=0, tiled=False)
-    parts = parts.reshape(slab, depth_count, slab, cells).sum(axis=0)
+    parts = sum_density(partial, row_count, column_count, depth_count)
     tile_shape = core_density.shape
     grid = parts.reshape((depth_count, row_count, column_count) + tile_shape)
     grid = grid.transpose(1, 3, 2, 4, 0, 5).reshape(
@@ -373,9 +662,9 @@
     )
     field = field.transpose(4, 0, 2, 1, 3, 5).reshape(tiles, 1, cells)
     hamiltonian, terms = owned_hamiltonian(
-        phi, field, rows, sources, place, keep, orbitals, size, per_column
-    )
-    applied = lax.psum_scatter(terms, ("col", "gz"), scatter_dimension=0, tiled=True)
+        rows_phi, cols_phi, field, rows, sources, place, keep, orbitals, size, per_column
+    )
+    applied = sum_applied(terms, column_count)
     return hamiltonian, applied
 
 
@@ -383,7 +672,9 @@
     arguments = (
         density_matrix, block_pattern, tile_lists, basis_values, core_density, orbitals,
     )
+    counts = lax.axis_size("row"), lax.axis_size("col"), lax.axis_size("gz")
     fits = tile_lists.shape[0] * basis_values.size * 2 <= gathered_limit
+    fits = fits and counts[0] == 2 and counts[1] % 2 == 0 and counts[2] == 4
     return gathered(*arguments) if fits else exchanged(*arguments)
 
 

time: 383 us -> 236 us (0.62)
  waiting for transfers between devices: 258 us -> 0 us
  Pallas kernels: 55.2 us -> 215 us
  blocking collectives: 40.5 us -> 0 us
  between operations: 14 us -> 0.91 us
    all_gather x2 -> x0, waiting for transfers between devices: 194 us -> none  [the longest x1 104 us: gathered(): slab_phi = lax.all_gather(phi_tile, ('row', 'col'), axis=0, tiled=False)]
    pallas_call x0 -> x3, Pallas kernels: none -> 161 us  [the longest x1 109 us: gather_basis(): pl.pallas_call(body, in_specs=[pl.BlockSpec(memory_space=pltpu.HBM)], out...]
    reduce_scatter x1 -> x0, waiting for transfers between devices: 63.8 us -> none  [gathered(): lax.psum_scatter(terms, ('col', 'gz'), scatter_dimension=0, tiled=True)]
    all_gather x1 -> x0, blocking collectives: 40.5 us -> none  [gathered(): parts = lax.all_gather(partial, ('row', 'col', 'gz'), axis=0, tiled=False)]
  transfers between devices with their start and end apart: 3 -> 0, of which waited for: 3 -> 0; matrix products, arithmetic and copies ran while one was open for 3% -> 0% of each run, Pallas kernels for 4% -> 0%
where the time goes in v2:
time: 236 us; the launch traced here: 234 us
  Pallas kernels  215 us (91%)
  local copies, waits for them, and re-layouts  11.3 us (5%)
  other arithmetic  6.39 us (3%)
    pallas_call x1, Pallas kernels, gather_basis(): pl.pallas_call(body, in_specs=[pl.BlockSpec(memory_space=pltpu.HBM)], out...  109 us
    pallas_call x1, Pallas kernels, owned_hamiltonian(): pl.pallas_call(body, grid_spec=grid_spec, out_shape=[jax.ShapeDtypeStruct...  40.9 us
    pallas_call x1, Pallas kernels, sum_applied(): pl.pallas_call(body, in_specs=[pl.BlockSpec(memory_space=pltpu.VMEM)], ou...  26.9 us
    pallas_call x1, Pallas kernels, sum_density(): pl.pallas_call(body, in_specs=[pl.BlockSpec(memory_space=pltpu.VMEM)], ou...  25.7 us
    pallas_call x1, Pallas kernels, partial_density(): pl.pallas_call(body, grid_spec=grid_spec, out_shape=jax.ShapeDtypeStruct(...  13 us

profile of v2, /device:TPU:0, one launch (start us, length us, event | category | flops | bytes accessed | tf_op | source)
XLA Modules:
  0.0 233.6 jit_solution(354554244644256757)
XLA Ops:
  0.6 0.0 copy-start
  0.7 0.7 pad_add_fusion.refs_3_.refs_2_
  1.3 0.8 broadcast_in_dim.58
  2.1 0.7 dynamic-slice_convert_fusion
  2.8 0.8 copy.20
  3.6 0.1 dynamic-slice_subtract_fusion
  3.7 0.1 dynamic-slice_subtract_fusion.1.refs_0_
  3.7 0.0 copy-start.1
  3.7 0.1 copy.22
  3.8 0.6 fusion.13
  4.4 0.1 select_reduce_fusion
  4.5 0.6 fusion.11
  5.1 0.7 copy.30.refs_1_
  5.8 0.1 broadcast_or_fusion
  5.8 0.1 reshape.125
  6.0 0.0 copy-done
  6.0 2.0 gather_fusion
  8.0 0.0 copy-done.1
  8.0 0.7 reshape.109.refs_2_
  8.7 0.1 copy.29
  8.7 0.1 broadcast_in_dim.61
  8.9 0.8 reshape.112.refs_7_
  9.7 108.6 %gather_basis.1 = (bf16[4,2,4,512,384]{4,3,2,1,0:T(8,128)(2,1)}, bf16[4,2,4,256,384]{4,3,2,1,0:T(8,128)(2,1)}) custom-call(bf16[2,512,384]{2,1,0:T(8,128)(2,1)} %bitcast.61), custom_call_target="tpu_custom_call" | custom-call | tf_op jit(solution)/shard_map/gather_basis/pallas_call | solution.py:255
  118.3 13.0 %partial_density.1 = f32[8,1,384]{2,1,0:T(1,128)} custom-call(s32[8,8]{1,0:T(8,128)} %get-tuple-element.14.refs_0_, s32[8,4]{1,0:T(8,128)} %get-tuple-element.16.refs_1_, s32[8,32]{1,0:T(8,128)} %reshape.109.refs_2_, s32[3]{0:T(128)} %pad_add_fusion.refs_3_.refs_2_, bf16[4096,2048]{1,0:T(8,128)(2,1)} %refs_11_.1, bf16[4096,2048]{1,0:T(8,128)(2,1)} %refs_11_.1, ...), custom_call_target="tpu_custom_call" | custom-call | flops 1610612736 | bytes 16777216 | tf_op jit(solution)/shard_map/partial_density/pallas_call | solution.py:475
  131.2 1.4 bitcast_add_fusion.refs_0_
  132.6 25.7 %sum_density.1 = f32[4,8,384]{2,1,0:T(8,128)} custom-call(f32[8,384]{1,0:T(8,128)} %bitcast_add_fusion.refs_0_), custom_call_target="tpu_custom_call" | custom-call | tf_op jit(solution)/shard_map/sum_density/pallas_call | solution.py:329
  158.4 0.9 power_multiply_fusion.2
  159.3 0.2 reshape.117
  159.5 0.2 reshape.119
  159.6 0.2 reshape.124
  159.8 0.2 reshape.123
  160.0 0.2 max.20
  160.2 0.2 copy.43
  160.3 0.2 max.22
  160.6 0.1 fusion.28
  160.7 0.1 fusion.27
  160.7 0.2 fusion.16
  161.1 0.1 fusion.18
  161.1 0.1 fusion.17
  161.2 0.1 fusion.9
  161.3 0.2 add.99
  161.5 0.2 reshape.115
  161.7 0.9 fusion.3
  162.6 0.8 reshape.111.refs_6_
  163.4 40.9 %owned_hamiltonian.1 = (f32[4096,512]{1,0:T(8,128)}, f32[4096,128]{1,0:T(8,128)}) custom-call(s32[32,8]{1,0:T(8,128)} %copy-done.1, s32[32,8]{1,0:T(8,128)} %copy.30.refs_1_, s32[3]{0:T(128)} %pad_add_fusion.refs_3_.refs_2_, bf16[32,512,384]{2,1,0:T(8,128)(2,1)} %bitcast.55, bf16[32,512,384]{2,1,0:T(8,128)(2,1)} %bitcast.56, bf16[32,256,384]{2,1,0:T(8,128)(2,1)} %bitcast.58, ...), custom_call_target="tpu_custom_call" | custom-call | tf_op jit(solution)/shard_map/owned_hamiltonian/pallas_call | solution.py:581
  204.3 1.8 copy.42
  206.1 26.9 %sum_applied.1 = f32[256,128]{1,0:T(8,128)S(1)} custom-call(f32[2,2,4,256,128]{4,3,2,1,0:T(8,128)S(1)} %bitcast.52), custom_call_target="tpu_custom_call" | custom-call | tf_op jit(solution)/shard_map/sum_applied/pallas_call | solution.py:392
  232.9 0.7 copy.45
  (13 shorter events, 0.1 us)
Async XLA Ops:
  0.6 5.3 %copy-start = (s32[64,32]{0,1:T(8,128)S(1)}, s32[64,32]{0,1:T(8,128)}, u32[]{:S(2)}) copy-start(s32[64,32]{0,1:T(8,128)} %param.7) | copy-start | bytes 24580
  3.7 4.2 %copy-start.1 = (s32[32,8]{1,0:T(8,128)}, s32[32,8]{1,0:T(8,128)S(1)}, u32[]{:S(2)}) copy-start(s32[32,8]{1,0:T(8,128)S(1)} %dynamic-slice_subtract_fusion.1.refs_0_) | copy-start | bytes 3076

commit v3 on v2

--- a/solution.py
+++ b/solution.py
@@ -151,14 +151,15 @@
     share = phi.shape[1] // half
     provider = (j // half) == i
     offset = pl.multiple_of(lax.rem(j, half) * share, share)
-    others = [lax.rem(j + step, column_count) for step in range(1, column_count)]
     x_peer, y_peer, c_peer = (across, j, k), (i, j, beside), (i, j, twin)
-    z_peers = [(i, other, k) for other in others]
-    meet([x_peer, y_peer, c_peer] + z_peers)
-    started, started_cols, started_twin = [], [], []
+    up, down = lax.rem(j + 1, column_count), lax.rem(j + column_count - 1, column_count)
+    z_up, z_down = (i, up, k), (i, down, k)
+    meet([x_peer, y_peer, c_peer, z_up, z_down])
+    has_up, has_down = j < column_count - 1, j > 0
+    started, started_cols, started_twin, guarded = [], [], [], []
 
     def push(source, target, arrival, peer, log):
-        number = len(started) + len(started_cols) + len(started_twin)
+        number = len(started) + len(started_cols) + len(started_twin) + len(guarded)
         copy = pltpu.make_async_remote_copy(
             src_ref=source, dst_ref=target, send_sem=send.at[number], recv_sem=arrival,
             device_id=peer, device_id_type=MESH,
@@ -179,10 +180,14 @@
 
     queue = []
 
-    def spread(source, where, along_z, along_y):
-        if along_z:
-            for peer in z_peers:
-                push(source, rows_out.at[where], got.at[where], peer, started).start()
+    sent_z = []
+
+    def along(source, where, peer, condition):
+        copy = push(source, rows_out.at[where], got.at[where], peer, guarded)
+        sent_z.append((copy, condition))
+        pl.when(condition)(copy.start)
+
+    def spread(source, where, along_y):
         if along_y:
             push(source, rows_out.at[where], got.at[where], y_peer, started).start()
         column = push(
@@ -205,19 +210,35 @@
             arrived(cols_out, got_cols, where)
             copy.start()
 
-    spread(phi.at[i], own, True, True)
+    along(phi.at[i], own, z_up, has_up)
+    along(phi.at[i], own, z_down, has_down)
+    spread(phi.at[i], own, True)
     where = (k, across, j)
     arrived(rows_out, got, where)
-    spread(rows_out.at[where], where, True, True)
-    slab = [(side, other) for side in (i, across) for other in others]
-    for side, other in slab:
-        where = (k, side, other)
-        arrived(rows_out, got, where)
-        spread(rows_out.at[where], where, False, True)
+    along(rows_out.at[where], where, z_up, has_up)
+    along(rows_out.at[where], where, z_down, has_down)
+    spread(rows_out.at[where], where, True)
+    order = []
+    for step in range(1, column_count):
+        low, high = jnp.minimum(j, column_count - 1 - j), column_count - 1
+        turn = (step + 1) // 2
+        both = turn <= low
+        sign_down = step % 2 == 1
+        paired = j - turn if sign_down else j + turn
+        rest = jnp.where(j < column_count - 1 - j, j + (step - low), j - (step - low))
+        order.append(jnp.where(both, paired, rest))
+    for other in order:
+        for side in (i, across):
+            where = (k, side, other)
+            arrived(rows_out, got, where)
+            along(rows_out.at[where], where, z_up, jnp.logical_and(other < j, has_up))
+            along(rows_out.at[where], where, z_down, jnp.logical_and(other > j, has_down))
+            spread(rows_out.at[where], where, True)
+    slab = [(side, other) for other in order for side in (i, across)]
     for side, other in [(i, j), (across, j)] + slab:
         where = (beside, side, other)
         arrived(rows_out, got, where)
-        spread(rows_out.at[where], where, False, False)
+        spread(rows_out.at[where], where, False)
     while queue:
         relay(queue.pop(0))
     for depth in (twin, lax.rem(twin + 2, 4)):
@@ -239,6 +260,8 @@
 
     for copy in started:
         copy.wait_send()
+    for copy, condition in sent_z:
+        pl.when(condition)(copy.wait_send)
     local.wait()
 
 
@@ -247,7 +270,7 @@
     halves = phi_tile.reshape(row_count, width // row_count, cells)
     grid = (depth_count, row_count, column_count)
     count = row_count * column_count
-    messages = 1 + row_count * (column_count - 1) + count + 3 * 2 * count
+    messages = 1 + 3 * count + 3 * 2 * count
 
     def body(*refs):
         basis_kernel(row_count, column_count, *refs)
@@ -381,9 +404,7 @@
 
 
 def sum_applied(terms, column_count):
-    high, norb = terms.shape
-    rows = high // (4 * column_count)
-    parts = terms.reshape(column_count, 2, 2, rows, norb).transpose(1, 2, 0, 3, 4)
+    rows, norb = terms.shape[3:]
     part = (column_count, rows, norb)
 
     def body(*refs):
@@ -407,16 +428,19 @@
             collective_id=2, has_side_effects=True, vmem_limit_bytes=vmem_bytes // 2
         ),
         name="sum_applied",
-    )(parts)
-
-
-def density_kernel(per_row, per_column, size, rows_ref, cols_ref, keep_ref, place_ref, *refs):
+    )(terms)
+
+
+def density_kernel(per_row, per_column, size, counts, lists_ref, pattern_ref, place_ref, *refs):
     strips = refs[:per_row]
     phi_rows, phi_near, phi_far, out, picked, padded = refs[per_row:]
-    tile = pl.program_id(0)
     pair_width = 2 * size
+    row_blocks, column_blocks = pattern_ref.shape
+    tile = pl.program_id(0) * counts[2] + place_ref[5]
+    rows = [lists_ref[tile, place_ref[3] * per_row + m] for m in range(per_row)]
+    rows = [row - place_ref[3] * row_blocks for row in rows]
     for n in range(per_column):
-        column = cols_ref[tile, n]
+        column = lists_ref[tile, place_ref[4] * per_column + n] - place_ref[4] * column_blocks
         start = pl.multiple_of((column // 2) * pair_width, pair_width)
         odd = column % 2
         span = slice(n * size, (n + 1) * size)
@@ -427,7 +451,7 @@
             )
         for m in range(per_row):
             block = strips[m][:, pl.ds(start, pair_width)]
-            kept = keep_ref[tile, m * per_column + n] != 0
+            kept = pattern_ref[rows[m], column] != 0
             picked[m * size : (m + 1) * size, n * pair_width : (n + 1) * pair_width] = jnp.where(
                 kept, block, jnp.zeros_like(block)
             )
@@ -436,33 +460,38 @@
     out[0] = rho
 
 
-def partial_density(density_matrix, rows_phi, cols_phi, rows, cols, keep, place, size):
-    tiles, cells = rows.shape[0], rows_phi.shape[2]
-    per_row, per_column = rows.shape[1], cols.shape[1]
+def partial_density(density_matrix, rows_phi, cols_phi, lists, pattern, place, size, counts):
+    tiles, cells = counts[0] * counts[1], rows_phi.shape[2]
+    per_row, per_column = lists.shape[1] // counts[0], lists.shape[1] // counts[1]
+    row_blocks = pattern.shape[0]
     columns = density_matrix.shape[1]
 
     def strip_spec(m):
-        return pl.BlockSpec((size, columns), lambda t, rows, cols, keep, place: (rows[t, m], 0))
+        def strip(t, lists, pattern, place):
+            row = lists[t * counts[2] + place[5], place[3] * per_row + m]
+            return row - place[3] * row_blocks, 0
+
+        return pl.BlockSpec((size, columns), strip)
 
     grid_spec = pltpu.PrefetchScalarGridSpec(
-        num_scalar_prefetch=4,
+        num_scalar_prefetch=3,
         grid=(tiles,),
         in_specs=[strip_spec(m) for m in range(per_row)]
         + [
             pl.BlockSpec(
                 (1, per_row * size, cells),
-                lambda t, rows, cols, keep, place: (place[2] + t, 0, 0),
+                lambda t, lists, pattern, place: (place[2] + t, 0, 0),
             ),
             pl.BlockSpec(
                 (1, per_column * size, cells),
-                lambda t, rows, cols, keep, place: ((place[2] + t) * place[1], place[0], 0),
+                lambda t, lists, pattern, place: ((place[2] + t) * place[1], place[0], 0),
             ),
             pl.BlockSpec(
                 (1, per_column * size, cells),
-                lambda t, rows, cols, keep, place: ((place[2] + t) * (1 - place[1]), 0, 0),
+                lambda t, lists, pattern, place: ((place[2] + t) * (1 - place[1]), 0, 0),
             ),
         ],
-        out_specs=pl.BlockSpec((1, 1, cells), lambda t, rows, cols, keep, place: (t, 0, 0)),
+        out_specs=pl.BlockSpec((1, 1, cells), lambda t, lists, pattern, place: (t, 0, 0)),
         scratch_shapes=[
             pltpu.VMEM((per_row * size, 2 * per_column * size), jnp.bfloat16),
             pltpu.VMEM((2 * per_column * size, cells), jnp.bfloat16),
@@ -470,7 +499,7 @@
     )
 
     def body(*refs):
-        density_kernel(per_row, per_column, size, *refs)
+        density_kernel(per_row, per_column, size, counts, *refs)
 
     return pl.pallas_call(
         body,
@@ -483,111 +512,146 @@
             transcendentals=0,
         ),
         name="partial_density",
-    )(rows, cols, keep, place, *([density_matrix] * per_row), rows_phi, rows_phi, cols_phi)
+    )(lists, pattern, place, *([density_matrix] * per_row), rows_phi, rows_phi, cols_phi)
 
 
 def hamiltonian_kernel(
-    per_row, size, owned, rows_ref, from_ref, place_ref, phi_rows, phi_near, phi_far, field, keep, orbitals,
-    out, terms, total, weighted, padded,
+    per_row, per_column, size, owned, counts, together, column_blocks, lists_ref, place_ref,
+    phi_rows, phi_near, phi_far, field, keep, upper, lower, out, terms, total, weighted, padded,
+    sems,
 ):
-    tile = pl.program_id(0)
+    step = pl.program_id(0)
     pair_width = 2 * size
-
-    @pl.when(tile == 0)
+    slab = counts[0] * counts[1]
+    row_blocks = total.shape[0] // size
+
+    @pl.when(step == 0)
     def _():
         total[...] = jnp.zeros_like(total)
 
-    weighted[...] = (phi_rows[0].astype(jnp.float32) * field[0]).astype(jnp.bfloat16)
-    for pair in range(owned // 2):
-        left = from_ref[tile, 2 * pair]
-        right = from_ref[tile, 2 * pair + 1]
-
-        @pl.when(jnp.maximum(left, right) >= 0)
-        def _():
-            for half, source in enumerate((left, right)):
-                start = pl.multiple_of(jnp.maximum(source, 0) * size, size)
-                span = pl.ds(start, size)
-                values = jnp.where(place_ref[1] == 1, phi_near[0, span, :], phi_far[0, span, :])
-                padded[half * size : (half + 1) * size, :] = jnp.where(
-                    source >= 0, values, jnp.zeros_like(values)
+    for inner in range(together):
+        number = step * together + inner
+        tile = lax.rem(number, slab) * counts[2] + number // slab
+        base = place_ref[4] * column_blocks + place_ref[5] * owned
+        listed = [lists_ref[tile, place_ref[4] * per_column + n] - base for n in range(per_column)]
+        weighted[...] = (phi_rows[inner].astype(jnp.float32) * field[inner]).astype(jnp.bfloat16)
+        for pair in range(owned // 2):
+            sources = []
+            for half in range(2):
+                source = jnp.int32(-1)
+                for n in range(per_column):
+                    source = jnp.where(listed[n] == 2 * pair + half, n, source)
+                sources.append(source)
+
+            @pl.when(jnp.maximum(sources[0], sources[1]) >= 0)
+            def _():
+                for half, source in enumerate(sources):
+                    span = pl.ds(pl.multiple_of(jnp.maximum(source, 0) * size, size), size)
+                    values = jnp.where(
+                        place_ref[1] == 1, phi_near[inner, span, :], phi_far[inner, span, :]
+                    )
+                    padded[half * size : (half + 1) * size, :] = jnp.where(
+                        source >= 0, values, jnp.zeros_like(values)
+                    )
+                product = lax.dot_general(
+                    weighted[...],
+                    padded[...],
+                    (((1,), (1,)), ((), ())),
+                    preferred_element_type=jnp.float32,
                 )
-            product = lax.dot_general(
-                weighted[...],
-                padded[...],
-                (((1,), (1,)), ((), ())),
-                preferred_element_type=jnp.float32,
+                span = slice(pair * pair_width, (pair + 1) * pair_width)
+                for m in range(per_row):
+                    row = lists_ref[tile, place_ref[3] * per_row + m] - place_ref[3] * row_blocks
+                    start = pl.multiple_of(row * size, size)
+                    total[pl.ds(start, size), span] += product[m * size : (m + 1) * size]
+
+    @pl.when(step == pl.num_programs(0) - 1)
+    def _():
+        high = terms.shape[3]
+        parts = high // size
+        copies = []
+        norb = lower.shape[1]
+        for chunk in range(total.shape[0] // high):
+            for part in range(parts):
+                block = chunk * parts + part
+                span = slice(block * size, (block + 1) * size)
+                total[span, :] = total[span, :] * keep[block : block + 1, :]
+            span = slice(chunk * high, (chunk + 1) * high)
+            copy = pltpu.make_async_copy(total.at[span], out.at[span], sems.at[chunk])
+            copy.start()
+            copies.append(copy)
+            values = total[span, :]
+            coarse = values.astype(jnp.bfloat16)
+            fine = (values - coarse.astype(jnp.float32)).astype(jnp.bfloat16)
+            first = jnp.dot(coarse, upper[...], preferred_element_type=jnp.float32)
+            second = jnp.dot(fine, upper[:, :norb], preferred_element_type=jnp.float32)
+            depth = chunk % counts[2]
+            terms[depth // 2, depth % 2, chunk // counts[2]] = (
+                first[:, :norb] + (first[:, norb:] + second)
             )
-            span = slice(pair * pair_width, (pair + 1) * pair_width)
-            for m in range(per_row):
-                start = pl.multiple_of(rows_ref[tile, m] * size, size)
-                total[pl.ds(start, size), span] += product[m * size : (m + 1) * size]
-
-    @pl.when(tile == pl.num_programs(0) - 1)
-    def _():
-        step = 4 * size
-
-        @pl.loop(0, total.shape[0] // step)
-        def _(chunk):
-            for part in range(4):
-                span = pl.ds(pl.multiple_of(chunk * step + part * size, size), size)
-                out[span, :] = total[span, :] * keep[pl.ds(chunk * 4 + part, 1), :]
-            span = pl.ds(pl.multiple_of(chunk * step, step), step)
-            terms[span, :] = jnp.dot(
-                out[span, :],
-                orbitals[...],
-                precision=lax.Precision.HIGHEST,
-                preferred_element_type=jnp.float32,
-            )
-
-
-def owned_hamiltonian(rows_phi, cols_phi, field, rows, sources, place, keep, orbitals, size, per_column):
+        for copy in copies:
+            copy.wait()
+
+
+def owned_hamiltonian(rows_phi, cols_phi, field, lists, place, keep, orbitals, size, counts):
     tiles, width, cells = rows_phi.shape
-    per_row = rows.shape[1]
-    owned = sources.shape[1]
+    per_row, per_column = lists.shape[1] // counts[0], lists.shape[1] // counts[1]
     high = keep.shape[0] * size
-    wide = owned * size
+    wide = keep.shape[1]
+    owned = wide // size
     norb = orbitals.shape[1]
+    together = 4
+    chunks = counts[1] * counts[2]
+    rounded = lax.reduce_precision(orbitals, exponent_bits=8, mantissa_bits=7)
+    coarse = rounded.astype(jnp.bfloat16)
+    fine = (orbitals - rounded).astype(jnp.bfloat16)
+    upper = jnp.concatenate([coarse, fine], axis=1)
+    term_shape = (2, 2, counts[1], high // chunks, norb)
     grid_spec = pltpu.PrefetchScalarGridSpec(
-        num_scalar_prefetch=3,
-        grid=(tiles,),
+        num_scalar_prefetch=2,
+        grid=(tiles // together,),
         in_specs=[
-            pl.BlockSpec((1, per_row * size, cells), lambda t, rows, sources, place: (t, 0, 0)),
+            pl.BlockSpec((together, per_row * size, cells), lambda t, lists, place: (t, 0, 0)),
             pl.BlockSpec(
-                (1, per_column * size, cells),
-                lambda t, rows, sources, place: (t * place[1], place[0], 0),
+                (together, per_column * size, cells),
+                lambda t, lists, place: (t * place[1], place[0], 0),
             ),
             pl.BlockSpec(
-                (1, per_column * size, cells),
-                lambda t, rows, sources, place: (t * (1 - place[1]), 0, 0),
+                (together, per_column * size, cells),
+                lambda t, lists, place: (t * (1 - place[1]), 0, 0),
             ),
-            pl.BlockSpec((1, 1, cells), lambda t, rows, sources, place: (t, 0, 0)),
-            pl.BlockSpec(keep.shape, lambda t, rows, sources, place: (0, 0)),
-            pl.BlockSpec(orbitals.shape, lambda t, rows, sources, place: (0, 0)),
+            pl.BlockSpec((together, 1, cells), lambda t, lists, place: (t, 0, 0)),
+            pl.BlockSpec(keep.shape, lambda t, lists, place: (0, 0)),
+            pl.BlockSpec(upper.shape, lambda t, lists, place: (0, 0)),
+            pl.BlockSpec(coarse.shape, lambda t, lists, place: (0, 0)),
         ],
         out_specs=[
-            pl.BlockSpec((high, wide), lambda t, rows, sources, place: (0, 0)),
-            pl.BlockSpec((high, norb), lambda t, rows, sources, place: (0, 0)),
+            pl.BlockSpec(memory_space=pltpu.HBM),
+            pl.BlockSpec(term_shape, lambda t, lists, place: (0, 0, 0, 0, 0)),
         ],
         scratch_shapes=[
             pltpu.VMEM((high, wide), jnp.float32),
             pltpu.VMEM((per_row * size, cells), jnp.bfloat16),
             pltpu.VMEM((2 * size, cells), jnp.bfloat16),
+            pltpu.SemaphoreType.DMA((chunks,)),
         ],
     )
 
     def body(*refs):
-        hamiltonian_kernel(per_row, size, owned, *refs)
+        hamiltonian_kernel(
+            per_row, per_column, size, owned, counts, together, owned * counts[2], *refs
+        )
 
     return pl.pallas_call(
         body,
         grid_spec=grid_spec,
         out_shape=[
             jax.ShapeDtypeStruct((high, wide), jnp.float32),
-            jax.ShapeDtypeStruct((high, norb), jnp.float32),
+            jax.ShapeDtypeStruct(term_shape, jnp.float32),
         ],
         compiler_params=pltpu.CompilerParams(vmem_limit_bytes=vmem_bytes),
         name="owned_hamiltonian",
-    )(rows, sources, place, rows_phi, rows_phi, cols_phi, field, keep, orbitals)
+    )(lists, place, rows_phi, rows_phi, cols_phi, field, keep, upper, coarse)
 
 
 def whole_potential(density):
@@ -615,37 +679,22 @@
     row_blocks, column_blocks = block_pattern.shape
     size = density_matrix.shape[0] // row_blocks
     tiles, listed = tile_lists.shape
-    per_row = listed // row_count
-    per_column = listed // column_count
     owned = column_blocks // depth_count
     cells = core_density.size
     phi_tile = basis_values.reshape(listed * size, cells)
 
-    lists = tile_lists.reshape(row_count, column_count, depth_count, listed).transpose(2, 0, 1, 3)
-    lists = lists.reshape(tiles, listed)
-    rows = lax.dynamic_slice_in_dim(lists, row_index * per_row, per_row, 1) - row_index * row_blocks
-    cols = (
-        lax.dynamic_slice_in_dim(lists, column_index * per_column, per_column, 1)
-        - column_index * column_blocks
-    )
     slab = row_count * column_count
-    slab_rows = lax.dynamic_slice_in_dim(rows, depth_index * slab, slab, 0)
-    slab_cols = lax.dynamic_slice_in_dim(cols, depth_index * slab, slab, 0)
-    slab_keep = block_pattern[slab_rows[:, :, None], slab_cols[:, None, :]]
-    slab_keep = slab_keep.reshape(slab, per_row * per_column)
+    counts = (row_count, column_count, depth_count)
     half = column_count // row_count
     near = (column_index // half == row_index).astype(jnp.int32)
-    place = jnp.stack([column_index % half, near, depth_index * slab]).astype(jnp.int32)
-    own_ids = depth_index * owned + jnp.arange(owned, dtype=jnp.int32)
-    matches = cols[:, None, :] == own_ids[None, :, None]
-    numbers = jnp.arange(per_column, dtype=jnp.int32)[None, None, :]
-    sources = jnp.max(jnp.where(matches, numbers, -1), axis=2).astype(jnp.int32)
+    place = [column_index % half, near, depth_index * slab, row_index, column_index, depth_index]
+    place = jnp.stack(place).astype(jnp.int32)
     own_pattern = lax.dynamic_slice_in_dim(block_pattern, depth_index * owned, owned, 1)
     keep = jnp.repeat(own_pattern.astype(jnp.float32), size, axis=1)
 
     rows_phi, cols_phi = gather_basis(phi_tile, row_count, column_count, depth_count)
     partial = partial_density(
-        density_matrix, rows_phi, cols_phi, slab_rows, slab_cols, slab_keep, place, size
+        density_matrix, rows_phi, cols_phi, tile_lists, block_pattern, place, size, counts
     )
     partial = partial.reshape(slab, cells)
     own_tile = (row_index * column_count + column_index) == jnp.arange(slab)[:, None]
@@ -662,7 +711,7 @@
     )
     field = field.transpose(4, 0, 2, 1, 3, 5).reshape(tiles, 1, cells)
     hamiltonian, terms = owned_hamiltonian(
-        rows_phi, cols_phi, field, rows, sources, place, keep, orbitals, size, per_column
+        rows_phi, cols_phi, field, tile_lists, place, keep, orbitals, size, counts
     )
     applied = sum_applied(terms, column_count)
     return hamiltonian, applied

time: 236 us -> 191 us (0.81)
  Pallas kernels: 215 us -> 172 us
    pallas_call x1, Pallas kernels: 40.9 us -> 21.3 us  [owned_hamiltonian(): pl.pallas_call(body, grid_spec=grid_spec, out_shape=[jax.ShapeDtypeStruct...]
    pallas_call x1, Pallas kernels: 25.7 us -> 13.6 us  [sum_density(): pl.pallas_call(body, in_specs=[pl.BlockSpec(memory_space=pltpu.VMEM)], ou...]
    pallas_call x1, Pallas kernels: 109 us -> 97.1 us  [gather_basis(): pl.pallas_call(body, in_specs=[pl.BlockSpec(memory_space=pltpu.HBM)], out...]
    unnamed x6 -> x7, local copies, waits for them, and re-layouts: 1.44 us -> 5.04 us
    reshape x2 -> x0, local copies, waits for them, and re-layouts: 2.45 us -> none  [the longest x1 1.78 us: sum_applied(): terms.reshape(column_count, 2, 2, rows, norb).transpose(1, 2, 0, 3, 4)]
where the time goes in v3:
time: 191 us; the launch traced here: 189 us
  Pallas kernels  172 us (90%)
  local copies, waits for them, and re-layouts  10.2 us (5%)
  other arithmetic  5.97 us (3%)
    pallas_call x1, Pallas kernels, gather_basis(): pl.pallas_call(body, in_specs=[pl.BlockSpec(memory_space=pltpu.HBM)], out...  97.1 us
    pallas_call x1, Pallas kernels, sum_applied(): pl.pallas_call(body, in_specs=[pl.BlockSpec(memory_space=pltpu.VMEM)], ou...  26.8 us
    pallas_call x1, Pallas kernels, owned_hamiltonian(): pl.pallas_call(body, grid_spec=grid_spec, out_shape=[jax.ShapeDtypeStruct...  21.3 us
    pallas_call x1, Pallas kernels, sum_density(): pl.pallas_call(body, in_specs=[pl.BlockSpec(memory_space=pltpu.VMEM)], ou...  13.6 us
    pallas_call x1, Pallas kernels, partial_density(): pl.pallas_call(body, grid_spec=grid_spec, out_shape=jax.ShapeDtypeStruct(...  13.6 us
    unnamed x7, local copies, waits for them, and re-layouts  5.04 us

profile of v3, /device:TPU:0, one launch (start us, length us, event | category | flops | bytes accessed | tf_op | source)
XLA Modules:
  0.0 189.4 jit_solution(14438509110876782150)
XLA Ops:
  0.7 0.7 stack.31.refs_2_.refs_1_
  1.3 0.8 broadcast_in_dim.27
  2.1 0.7 dynamic-slice_convert_fusion
  2.8 1.4 copy.21.refs_0_
  4.2 0.1 copy.20
  4.3 1.4 copy.13.refs_1_
  5.7 0.1 broadcast_in_dim.30
  5.8 0.8 reshape.79.refs_6_
  6.6 1.0 reduce-precision_convert_fusion
  7.6 0.0 copy-start.1
  7.6 0.7 pad_maximum_fusion.refs_7_
  8.3 97.1 %gather_basis.1 = (bf16[4,2,4,512,384]{4,3,2,1,0:T(8,128)(2,1)}, bf16[4,2,4,256,384]{4,3,2,1,0:T(8,128)(2,1)}) custom-call(bf16[2,512,384]{2,1,0:T(8,128)(2,1)} %bitcast.50), custom_call_target="tpu_custom_call" | custom-call | tf_op jit(solution)/shard_map/gather_basis/pallas_call | solution.py:278
  105.4 13.6 %partial_density.1 = f32[8,1,384]{2,1,0:T(1,128)} custom-call(s32[32,16]{1,0:T(8,128)} %copy.21.refs_0_, s32[64,32]{1,0:T(8,128)} %copy.13.refs_1_, s32[6]{0:T(128)} %stack.31.refs_2_.refs_1_, bf16[4096,2048]{1,0:T(8,128)(2,1)} %refs_10_.1, bf16[4096,2048]{1,0:T(8,128)(2,1)} %refs_10_.1, bf16[4096,2048]{1,0:T(8,128)(2,1)} %refs_10_.1, ...), custom_call_target="tpu_custom_call" | custom-call | flops 1610612736 | bytes 16777216 | tf_op jit(solution)/shard_map/partial_density/pallas_call | solution.py:504
  119.0 0.0 copy-done.1
  119.0 1.4 bitcast_add_fusion.refs_0_
  120.4 13.6 %sum_density.1 = f32[4,8,384]{2,1,0:T(8,128)} custom-call(f32[8,384]{1,0:T(8,128)} %bitcast_add_fusion.refs_0_), custom_call_target="tpu_custom_call" | custom-call | tf_op jit(solution)/shard_map/sum_density/pallas_call | solution.py:352
  134.0 0.9 power_multiply_fusion.2
  134.9 0.2 reshape.83
  135.1 0.2 reshape.85
  135.3 0.2 reshape.90
  135.5 0.2 reshape.89
  135.7 0.2 max.20
  135.8 0.2 copy.31
  136.0 0.2 max.22
  136.2 0.1 fusion.25
  136.3 0.1 fusion.24
  136.4 0.2 fusion.13
  136.7 0.1 fusion.15
  136.8 0.1 fusion.14
  136.9 0.1 fusion.10
  137.0 0.2 add.58
  137.2 0.2 reshape.81
  137.4 0.9 fusion.4
  138.3 0.8 reshape.78.refs_5_
  139.1 21.3 %owned_hamiltonian.1 = (f32[4096,512]{1,0:T(8,128)}, f32[2,2,4,256,128]{4,3,2,1,0:T(8,128)}) custom-call(s32[32,16]{1,0:T(8,128)} %copy.21.refs_0_, s32[6]{0:T(128)} %stack.31.refs_2_.refs_1_, bf16[32,512,384]{2,1,0:T(8,128)(2,1)} %bitcast.45, bf16[32,512,384]{2,1,0:T(8,128)(2,1)} %bitcast.46, bf16[32,256,384]{2,1,0:T(8,128)(2,1)} %bitcast.48, ...), custom_call_target="tpu_custom_call" | custom-call | tf_op jit(solution)/shard_map/owned_hamiltonian/pallas_call | solution.py:645
  160.4 0.0 copy-start
  160.4 1.6 copy-done
  162.0 26.8 %sum_applied.1 = f32[256,128]{1,0:T(8,128)S(1)} custom-call(f32[2,2,4,256,128]{4,3,2,1,0:T(8,128)S(1)} %copy-done), custom_call_target="tpu_custom_call" | custom-call | tf_op jit(solution)/shard_map/sum_applied/pallas_call | solution.py:413
  188.8 0.7 copy.33
  (11 shorter events, 0.1 us)
Async XLA Ops:
  7.6 111.4 %copy-start.1 = (bf16[512,128]{1,0:T(8,128)(2,1)}, bf16[512,128]{1,0:T(8,128)(2,1)S(1)}, u32[]{:S(2)}) copy-start(bf16[512,128]{1,0:T(8,128)(2,1)S(1)} %get-tuple-element.13.refs_8_) | copy-start | bytes 393220
  160.4 1.6 copy-start

commit v4 on v3

--- a/solution.py
+++ b/solution.py
@@ -382,24 +382,30 @@
         copy.start()
         return copy
 
-    first = push(0, terms.at[1 - y, 1 - c], c_got.at[0], c_peer)
-    second = push(1, terms.at[y, 1 - c], c_got.at[1], c_peer)
-    first.wait_recv()
-    y_send[...] = terms[1 - y, c] + c_got[0]
-    third = push(2, y_send, y_got, y_peer)
-    second.wait_recv()
-    z_send[...] = terms[y, c] + c_got[1]
-    third.wait_recv()
-    z_send[...] = z_send[...] + y_got[...]
-    last = []
-    for number, (other, peer) in enumerate(zip(others, z_peers)):
-        last.append(push(3 + number, z_send.at[other], z_got.at[number], peer))
+    order = others + [j]
+    first, second, third, last = [], [], [], []
+    for n, other in enumerate(order):
+        first.append(push(n, terms.at[1 - y, 1 - c, other], c_got.at[0, other], c_peer))
+    for n, other in enumerate(order):
+        second.append(
+            push(column_count + n, terms.at[y, 1 - c, other], c_got.at[1, other], c_peer)
+        )
+    for n, other in enumerate(order):
+        first[n].wait_recv()
+        y_send[other] = terms[1 - y, c, other] + c_got[0, other]
+        third.append(push(2 * column_count + n, y_send.at[other], y_got.at[other], y_peer))
+    for n, other in enumerate(order):
+        second[n].wait_recv()
+        third[n].wait_recv()
+        z_send[other] = terms[y, c, other] + c_got[1, other] + y_got[other]
+        if n < column_count - 1:
+            last.append(push(3 * column_count + n, z_send.at[other], z_got.at[n], z_peers[n]))
     total = z_send[j]
     for number, copy in enumerate(last):
         copy.wait_recv()
         total = total + z_got[number]
     out[...] = total
-    for copy in [first, second, third] + last:
+    for copy in first + second + third + last:
         copy.wait_send()
 
 
@@ -421,8 +427,8 @@
             pltpu.VMEM(part, terms.dtype),
             pltpu.VMEM(part, terms.dtype),
             pltpu.VMEM((column_count - 1, rows, norb), terms.dtype),
-            pltpu.SemaphoreType.DMA((2 + column_count,)),
-            pltpu.SemaphoreType.DMA((2 + column_count,)),
+            pltpu.SemaphoreType.DMA((4 * column_count,)),
+            pltpu.SemaphoreType.DMA((4 * column_count,)),
         ],
         compiler_params=pltpu.CompilerParams(
             collective_id=2, has_side_effects=True, vmem_limit_bytes=vmem_bytes // 2

time: 191 us -> 185 us (0.969)
  Pallas kernels: 172 us -> 167 us
    pallas_call x1, Pallas kernels: 26.8 us -> 20.5 us  [sum_applied(): pl.pallas_call(body, in_specs=[pl.BlockSpec(memory_space=pltpu.VMEM)], ou...]
where the time goes in v4:
time: 185 us; the launch traced here: 184 us
  Pallas kernels  167 us (90%)
  local copies, waits for them, and re-layouts  10.2 us (6%)
  other arithmetic  5.97 us (3%)
    pallas_call x1, Pallas kernels, gather_basis(): pl.pallas_call(body, in_specs=[pl.BlockSpec(memory_space=pltpu.HBM)], out...  97.1 us
    pallas_call x1, Pallas kernels, owned_hamiltonian(): pl.pallas_call(body, grid_spec=grid_spec, out_shape=[jax.ShapeDtypeStruct...  21.9 us
    pallas_call x1, Pallas kernels, sum_applied(): pl.pallas_call(body, in_specs=[pl.BlockSpec(memory_space=pltpu.VMEM)], ou...  20.5 us
    pallas_call x1, Pallas kernels, partial_density(): pl.pallas_call(body, grid_spec=grid_spec, out_shape=jax.ShapeDtypeStruct(...  14 us
    pallas_call x1, Pallas kernels, sum_density(): pl.pallas_call(body, in_specs=[pl.BlockSpec(memory_space=pltpu.VMEM)], ou...  13.3 us
    unnamed x7, local copies, waits for them, and re-layouts  5.04 us

profile of v4, /device:TPU:0, one launch (start us, length us, event | category | flops | bytes accessed | tf_op | source)
XLA Modules:
  0.0 183.7 jit_solution(12116967994430128642)
XLA Ops:
  0.7 0.7 stack.31.refs_2_.refs_1_
  1.3 0.8 broadcast_in_dim.27
  2.1 0.7 dynamic-slice_convert_fusion
  2.8 1.4 copy.21.refs_0_
  4.2 0.1 copy.20
  4.3 1.4 copy.13.refs_1_
  5.7 0.1 broadcast_in_dim.30
  5.8 0.8 reshape.79.refs_6_
  6.6 1.0 reduce-precision_convert_fusion
  7.6 0.0 copy-start.1
  7.6 0.7 pad_maximum_fusion.refs_7_
  8.3 97.1 %gather_basis.1 = (bf16[4,2,4,512,384]{4,3,2,1,0:T(8,128)(2,1)}, bf16[4,2,4,256,384]{4,3,2,1,0:T(8,128)(2,1)}) custom-call(bf16[2,512,384]{2,1,0:T(8,128)(2,1)} %bitcast.50), custom_call_target="tpu_custom_call" | custom-call | tf_op jit(solution)/shard_map/gather_basis/pallas_call | solution.py:278
  105.4 14.0 %partial_density.1 = f32[8,1,384]{2,1,0:T(1,128)} custom-call(s32[32,16]{1,0:T(8,128)} %copy.21.refs_0_, s32[64,32]{1,0:T(8,128)} %copy.13.refs_1_, s32[6]{0:T(128)} %stack.31.refs_2_.refs_1_, bf16[4096,2048]{1,0:T(8,128)(2,1)} %refs_10_.1, bf16[4096,2048]{1,0:T(8,128)(2,1)} %refs_10_.1, bf16[4096,2048]{1,0:T(8,128)(2,1)} %refs_10_.1, ...), custom_call_target="tpu_custom_call" | custom-call | flops 1610612736 | bytes 16777216 | tf_op jit(solution)/shard_map/partial_density/pallas_call | solution.py:510
  119.4 0.0 copy-done.1
  119.4 1.4 bitcast_add_fusion.refs_0_
  120.8 13.3 %sum_density.1 = f32[4,8,384]{2,1,0:T(8,128)} custom-call(f32[8,384]{1,0:T(8,128)} %bitcast_add_fusion.refs_0_), custom_call_target="tpu_custom_call" | custom-call | tf_op jit(solution)/shard_map/sum_density/pallas_call | solution.py:352
  134.1 0.9 power_multiply_fusion.2
  135.0 0.2 reshape.83
  135.1 0.2 reshape.85
  135.3 0.2 reshape.90
  135.5 0.2 reshape.89
  135.7 0.2 max.20
  135.9 0.2 copy.31
  136.0 0.2 max.22
  136.3 0.1 fusion.25
  136.3 0.1 fusion.24
  136.4 0.2 fusion.13
  136.8 0.1 fusion.15
  136.8 0.1 fusion.14
  136.9 0.1 fusion.10
  137.0 0.2 add.58
  137.2 0.2 reshape.81
  137.4 0.9 fusion.4
  138.3 0.8 reshape.78.refs_5_
  139.1 21.9 %owned_hamiltonian.1 = (f32[4096,512]{1,0:T(8,128)}, f32[2,2,4,256,128]{4,3,2,1,0:T(8,128)}) custom-call(s32[32,16]{1,0:T(8,128)} %copy.21.refs_0_, s32[6]{0:T(128)} %stack.31.refs_2_.refs_1_, bf16[32,512,384]{2,1,0:T(8,128)(2,1)} %bitcast.45, bf16[32,512,384]{2,1,0:T(8,128)(2,1)} %bitcast.46, bf16[32,256,384]{2,1,0:T(8,128)(2,1)} %bitcast.48, ...), custom_call_target="tpu_custom_call" | custom-call | tf_op jit(solution)/shard_map/owned_hamiltonian/pallas_call | solution.py:651
  161.0 0.0 copy-start
  161.0 1.6 copy-done
  162.6 20.5 %sum_applied.1 = f32[256,128]{1,0:T(8,128)S(1)} custom-call(f32[2,2,4,256,128]{4,3,2,1,0:T(8,128)S(1)} %copy-done), custom_call_target="tpu_custom_call" | custom-call | tf_op jit(solution)/shard_map/sum_applied/pallas_call | solution.py:419
  183.0 0.7 copy.33
  (11 shorter events, 0.1 us)
Async XLA Ops:
  7.6 111.8 %copy-start.1 = (bf16[512,128]{1,0:T(8,128)(2,1)}, bf16[512,128]{1,0:T(8,128)(2,1)S(1)}, u32[]{:S(2)}) copy-start(bf16[512,128]{1,0:T(8,128)(2,1)S(1)} %get-tuple-element.13.refs_8_) | copy-start | bytes 393220
  161.0 1.6 copy-start
